TPU v7x, 512 devices: a whole 4x4x16 slice. The times are simulated.
512 devices in a mesh: dom: 64 (over z, x), head: 8 (over y, core).
Axes of the slice: x: 4, y: 4, z: 16, core: 2. Of those that a mesh axis runs over, the one named last changes fastest.
Arguments:
- features: bfloat16 [262144, 768], P(('dom', 'head')), may hold values from -6.5 to 6.5
- qkv_weight: bfloat16 [768, 1536], replicated, may hold values from -0.21650635 to 0.21650635
- out_weight: bfloat16 [512, 768], replicated, may hold values from -0.25 to 0.25
- attn_gain: float32 [768], replicated, may hold values from 0.1 to 1.9
- up_weight: bfloat16 [768, 1536], P(None, 'dom'), may hold values from -0.21875 to 0.21875
- down_weight: bfloat16 [1536, 768], P('dom'), may hold values from -0.15625 to 0.15625
- final_gain: float32 [768], replicated, may hold values from 0.1 to 1.9
- node_order: int32 [262144], P('dom'), may hold values from 0 to 262143, as said below
- dest_part: int32 [2048, 2], P('dom'), may hold values from 0 to 63, all different within a row; in each aligned block of 32 rows (0 to 31, 32 to 63, ...) at most 2 rows name the same one
- key_block: int32 [2048, 2], P('dom'), may hold values from 0 to 31
- row_count: int32 [2048], P('dom'), may hold values from 16 to 128, as said below
Outputs:
- output: bfloat16 [262144, 768], P(('dom', 'head'))
Inputs may be any that keep to these rules, and one draw needn't show every extreme that they name: The entries node_order[p * 4096] to node_order[(p + 1) * 4096 - 1] are the nodes p * 4096 to (p + 1) * 4096 - 1, each once. `dest_part`: the 2 entries of a row are different partitions. Among the 32 rows of one partition no partition is named more than 2 times, and one is named exactly 2 times in some partitions. `row_count`: some block has all 128 nodes valid.
All inputs are finite; a program needn't handle non-finite values.
Results may differ from a plain program's by a relative error of at most 0.014.
Values may be sent and summed in bfloat16 or wider, within the bound.
A program may use at most 128 MiB of HBM per device.

v0:
```python
import math

import jax
import jax.numpy as jnp
from jax import lax
from jax.sharding import PartitionSpec as P

HEADS = 8
HD = 64
BLK = 128


def shortened(value):

    def short(part):
        return part.astype(jnp.bfloat16) if part.dtype == jnp.float32 else part

    return jax.tree.map(short, value)


def layer_norm(values, gain):
    centered = values - jnp.mean(values, -1, keepdims=True)
    spread = jnp.mean(centered * centered, -1, keepdims=True)
    return centered * lax.rsqrt(spread + 1e-05) * gain


def attend_core(query_blocks, key_blocks, value_blocks, key_count):
    head_width = query_blocks.shape[-1]
    scores = jnp.einsum(
        "pqhe,pkhe->phqk", query_blocks, key_blocks, preferred_element_type=jnp.float32
    ) * (1.0 / math.sqrt(head_width))
    positions = jnp.arange(key_blocks.shape[1], dtype=jnp.int32)
    kept_keys = positions[None, :] < key_count[:, None]
    scores = jnp.where(kept_keys[:, None, None, :], scores, -1e30)
    maxima = jnp.max(scores, -1)
    weights = jnp.exp(scores - maxima[..., None])
    totals = jnp.sum(weights, -1)
    summed = jnp.einsum(
        "phqk,pkhe->pqhe",
        weights.astype(jnp.bfloat16),
        value_blocks,
        preferred_element_type=jnp.float32,
    )
    partial_out = (summed / jnp.transpose(totals, (0, 2, 1))[..., None]).astype(jnp.bfloat16)
    return (maxima, totals, partial_out)


def attend(query_blocks, key_blocks, value_blocks, key_count):
    count_all = query_blocks.shape[0]
    groups = count_all // 8

    def grouped(packed):
        return attend_core(packed[0], packed[1], packed[2], packed[3])

    packed_all = (
        query_blocks.reshape((groups, 8) + query_blocks.shape[1:]),
        key_blocks.reshape((groups, 8) + key_blocks.shape[1:]),
        value_blocks.reshape((groups, 8) + value_blocks.shape[1:]),
        key_count.reshape(groups, 8),
    )
    results = lax.map(grouped, packed_all)
    return tuple(
        (result_part.reshape((count_all,) + result_part.shape[2:]) for result_part in results)
    )


def per_device(
    features,
    qkv_weight,
    out_weight,
    attn_gain,
    up_weight,
    down_weight,
    final_gain,
    node_order,
    dest_part,
    key_block,
    row_count,
):
    blocks = row_count.shape[0]
    listed = dest_part.shape[1]
    partitions = lax.axis_size("dom")
    capacity = max(2, 2 * blocks * listed // partitions)
    model_width = features.shape[1]
    local_heads = HEADS // lax.axis_size("head")
    projected = jnp.einsum(
        "rd,dck->crk",
        features,
        qkv_weight.reshape(model_width, 3, HEADS * HD),
        preferred_element_type=jnp.float32,
    ).astype(jnp.bfloat16)
    gathered = lax.all_to_all(projected, "head", split_axis=2, concat_axis=1, tiled=True)
    npart_rows = gathered.shape[1]
    local_order = node_order % npart_rows
    clustered = gathered[:, local_order, :].reshape(3, blocks, BLK, local_heads, HD)
    query_blocks = clustered[0]
    key_blocks = clustered[1]
    value_blocks = clustered[2]
    own_maxima, own_totals, own_out = attend(query_blocks, key_blocks, value_blocks, row_count)
    dest_flat = dest_part.reshape(-1)
    block_flat = key_block.reshape(-1)
    matches = (dest_flat[:, None] == jnp.arange(partitions, dtype=jnp.int32)[None, :]).astype(
        jnp.int32
    )
    before = jnp.cumsum(matches, 0) - matches
    slot_index = dest_flat * capacity + jnp.sum(before * matches, 1)
    slot_ids = jnp.arange(partitions * capacity, dtype=jnp.int32)
    selection = (slot_index[None, :] == slot_ids[:, None]).astype(jnp.int32)
    wanted = jnp.sum(selection * block_flat[None, :], 1).reshape(partitions, capacity)
    chosen = jnp.sum(selection.reshape(partitions * capacity, blocks, listed), 2).astype(
        jnp.bfloat16
    )
    outgoing = jnp.dot(
        chosen, query_blocks.reshape(blocks, -1), preferred_element_type=jnp.float32
    ).astype(jnp.bfloat16)
    outgoing = outgoing.reshape(partitions, capacity, -1)
    incoming = lax.all_to_all(outgoing, "dom", split_axis=0, concat_axis=0, tiled=True)
    requested = lax.all_to_all(wanted, "dom", split_axis=0, concat_axis=0, tiled=True)
    front_shape = (incoming.shape[0], incoming.shape[1])
    flat_requested = requested.reshape(-1)
    maxima, totals, partial_out = attend(
        incoming.reshape(-1, BLK, local_heads, HD),
        key_blocks[flat_requested],
        value_blocks[flat_requested],
        row_count[flat_requested],
    )
    partial_back, maxima_back, totals_back = (
        lax.all_to_all(
            shortened(partial_out.reshape(front_shape + (-1,))),
            "dom",
            split_axis=0,
            concat_axis=0,
            tiled=True,
        ),
        lax.all_to_all(
            shortened(maxima.reshape(front_shape + (-1,))),
            "dom",
            split_axis=0,
            concat_axis=0,
            tiled=True,
        ),
        lax.all_to_all(
            shortened(totals.reshape(front_shape + (-1,))),
            "dom",
            split_axis=0,
            concat_axis=0,
            tiled=True,
        ),
    )
    remote_out = partial_back.reshape(partitions * capacity, -1)[slot_index]
    remote_maxima = maxima_back.reshape(partitions * capacity, -1)[slot_index]
    remote_totals = totals_back.reshape(partitions * capacity, -1)[slot_index]
    all_maxima = jnp.concatenate(
        [own_maxima[:, None], remote_maxima.reshape(blocks, listed, local_heads, BLK)], 1
    )
    all_totals = jnp.concatenate(
        [own_totals[:, None], remote_totals.reshape(blocks, listed, local_heads, BLK)], 1
    )
    all_out = jnp.concatenate(
        [own_out[:, None], remote_out.reshape(blocks, listed, BLK, local_heads, HD)], 1
    )
    top_peak = jnp.max(all_maxima, 1)
    scale = all_totals * jnp.exp(all_maxima - top_peak[:, None])
    numer = jnp.sum(all_out.astype(jnp.float32) * jnp.transpose(scale, (0, 1, 3, 2))[..., None], 1)
    denom = jnp.transpose(jnp.sum(scale, 1), (0, 2, 1))[..., None]
    merged = numer / denom
    valid_rows = jnp.arange(BLK, dtype=jnp.int32)[None, :] < row_count[:, None]
    merged = jnp.where(valid_rows[:, :, None, None], merged, 0.0).astype(jnp.bfloat16)
    merged = merged.reshape(npart_rows, local_heads * HD)
    restored = jnp.zeros_like(merged).at[local_order].set(merged)
    node_heads = lax.all_to_all(restored, "head", split_axis=0, concat_axis=1, tiled=True)
    residual_sum = features.astype(jnp.float32) + jnp.dot(
        node_heads, out_weight, preferred_element_type=jnp.float32
    )
    hidden_norm = layer_norm(residual_sum, attn_gain).astype(jnp.bfloat16)
    hidden = jax.nn.gelu(
        jnp.dot(
            hidden_norm,
            lax.all_gather(up_weight, "dom", axis=1, tiled=True),
            preferred_element_type=jnp.float32,
        )
    ).astype(jnp.bfloat16)
    projected_back = jnp.dot(
        hidden,
        lax.all_gather(down_weight, "dom", axis=0, tiled=True),
        preferred_element_type=jnp.float32,
    )
    mixed = hidden_norm.astype(jnp.float32) + projected_back
    return layer_norm(mixed, final_gain).astype(jnp.bfloat16)


def solution(mesh):
    in_specs = (
        P(("dom", "head"), None),
        P(),
        P(),
        P(),
        P(None, "dom"),
        P("dom", None),
        P(),
        P("dom"),
        P("dom", None),
        P("dom", None),
        P("dom"),
    )
    out_specs = P(("dom", "head"), None)
    return jax.shard_map(
        per_device, mesh=mesh, in_specs=in_specs, out_specs=out_specs, check_vma=False
    )
```

profile of v0, /device:TPU:1, one launch (start us, length us, event | category | flops | bytes accessed | tf_op | source)
XLA Modules:
  0.0 551.4 jit_solution(5554872308989364258)
XLA Ops:
  6.5 2.9 copy.138
  9.5 2.6 fusion.48
  12.0 2.7 copy.139
  14.7 10.5 %all-to-all-start = ((bf16[3,512,512]{1,0,2:T(4,128)(2,1)}), bf16[3,512,512]{1,0,2:T(4,128)(2,1)S(1)}, u32[]{:S(2)}, u32[]{:S(2)}) async-start(bf16[3,512,512]{1,0,2:T(4,128)(2,1)} %copy.139), calls=%async_computation | async-start | bytes 4194304 | tf_op jit(solution)/shard_map/all_to_all | solution.py:92
  27.2 24.4 %all-to-all-done = bf16[3,512,512]{1,0,2:T(4,128)(2,1)S(1)} async-done(((bf16[3,512,512]{1,0,2:T(4,128)(2,1)}), bf16[3,512,512]{1,0,2:T(4,128)(2,1)S(1)}, u32[]{:S(2)}, u32[]{:S(2)}) %all-to-all-start) | async-done | bytes 1572896 | tf_op jit(solution)/shard_map/all_to_all | solution.py:92
  51.6 14.0 %all-to-all-start.1 = ((s32[64,1,2]{2,1,0:T(1,128)}), s32[64,1,2]{2,1,0:T(1,128)S(1)}, u32[]{:S(2)}, u32[]{:S(2)}) async-start(s32[64,1,2]{2,1,0:T(1,128)} %bitcast.27), calls=%async_computation.1 | async-start | bytes 65536 | tf_op jit(solution)/shard_map/all_to_all | solution.py:118
  65.6 2.3 copy.189
  67.9 5.7 %copy.170 = bf16[3,8,512,64]{3,0,2,1:T(4,128)(2,1)} copy(bf16[3,8,512,64]{2,1,3,0:T(8,128)(2,1)} %bitcast.186) | data formatting | bytes 3145728 | tf_op jit(solution)/shard_map/all_to_all | solution.py:92
  73.7 30.6 %gather_fusion = bf16[4096,3,64]{2,1,0:T(4,128)(2,1)} fusion(bf16[3,4096,64]{2,0,1:T(4,128)(2,1)} %bitcast.178, s32[4096]{0:T(1024)S(1)} %get-tuple-element.227), kind=kCustom, calls=%fused_computation | custom fusion | bytes 3162112 | tf_op jit(solution)/shard_map/gather | solution.py:95
  104.2 28.1 %fusion.71 = (bf16[1,4096,64]{2,0,1:T(2,128)(2,1)}, bf16[4096,64]{1,0:T(8,128)(2,1)S(1)}, bf16[1,4096,64]{2,0,1:T(2,128)(2,1)}, bf16[1,4096,64]{2,0,1:T(2,128)(2,1)}) fusion(bf16[3,4096,64]{2,0,1:T(4,128)(2,1)} %bitcast.177), kind=kLoop, calls=%fused_computation.130 | loop fusion | bytes 3670016 | tf_op jit(solution)/shard_map/slice | solution.py:96
  133.8 2.7 reshape.491
  136.5 14.8 %all-to-all-start.2 = ((bf16[64,2,8192]{2,1,0:T(2,128)(2,1)}), bf16[64,2,8192]{2,1,0:T(2,128)(2,1)}, u32[]{:S(2)}, u32[]{:S(2)}) async-start(bf16[64,2,8192]{2,1,0:T(2,128)(2,1)} %reshape.491), calls=%async_computation.2 | async-start | bytes 4194304 | tf_op jit(solution)/shard_map/all_to_all | solution.py:117
  158.9 2.7 copy.185
  163.2 2.2 gather_fusion.3
  165.4 82.9 %all-to-all-done.2 = bf16[64,2,8192]{2,1,0:T(2,128)(2,1)} async-done(((bf16[64,2,8192]{2,1,0:T(2,128)(2,1)}), bf16[64,2,8192]{2,1,0:T(2,128)(2,1)}, u32[]{:S(2)}, u32[]{:S(2)}) %all-to-all-start.2) | async-done | bytes 2097184 | tf_op jit(solution)/shard_map/all_to_all | solution.py:117
  248.3 7.9 %reshape_reshape.8 = bf16[16,8,128,1,64]{4,2,1,0,3:T(8,128)(2,1)} reshape(bf16[64,2,8192]{2,1,0:T(2,128)(2,1)} %all-to-all-done.2) | data formatting | bytes 4194304 | tf_op jit(solution)/shard_map/reshape;reshape | solution.py:56
  256.2 4.8 copy.158
  261.0 60.5 %while.29 = (s32[]{:T(128)}, bf16[16,8,1,128]{3,1,2,0:T(8,128)(2,1)S(1)}, bf16[16,8,1,128]{3,1,2,0:T(8,128)(2,1)}, bf16[16,8,128,1,64]{2,4,1,3,0:T(8,128)(2,1)},...) while((s32[]{:T(128)}, ...), condition=%wide.region_11.12_spmd, body=%wide.region_8.11_spmd.sunk | while | flops 34601984 | bytes 2138817 | solution.py:61
  266.2 1.8 fusion.103
  270.0 1.8 fusion.103
  273.8 1.8 fusion.103
  277.5 1.8 fusion.103
  281.3 1.8 fusion.103
  285.1 1.8 fusion.103
  288.9 1.8 fusion.103
  296.4 1.8 fusion.103
  300.2 1.8 fusion.103
  304.0 1.8 fusion.103
  307.8 1.8 fusion.103
  311.6 1.8 fusion.103
  319.1 1.8 fusion.103
  321.5 23.7 %all_to_all.66 = bf16[64,2,128]{2,1,0:T(2,128)(2,1)S(1)} all-to-all(bf16[64,2,128]{2,1,0:T(2,128)(2,1)S(1)} %bitcast.203), channel_id=1, replica_groups=mesh['dom'=64,'head'=8] {'dom'}, dimensions={0} | all-to-all | bytes 65536 | tf_op jit(solution)/shard_map/all_to_all | solution.py:135
  345.2 4.6 all-to-all-start.4
  349.8 4.8 copy.161
  354.5 7.9 %reshape_reshape.9 = bf16[64,2,8192]{2,1,0:T(2,128)(2,1)} reshape(bf16[16,8,128,1,64]{4,2,1,0,3:T(8,128)(2,1)} %copy.161) | data formatting | bytes 4194304 | tf_op jit(solution)/shard_map/reshape;reshape | solution.py:129
  363.2 14.1 %all-to-all-start.3 = ((bf16[64,2,8192]{2,1,0:T(2,128)(2,1)}), bf16[64,2,8192]{2,1,0:T(2,128)(2,1)}, u32[]{:S(2)}, u32[]{:S(2)}) async-start(bf16[64,2,8192]{2,1,0:T(2,128)(2,1)} %reshape_reshape.9), calls=%async_computation.3 | async-start | bytes 4194304 | tf_op jit(solution)/shard_map/all_to_all | solution.py:128
  380.0 1.8 copy.183
  382.2 6.8 %while.28 = (s32[]{:T(128)}, f32[4,8,1,128]{3,1,2,0:T(8,128)S(1)}, f32[4,8,1,128]{3,1,2,0:T(8,128)S(1)}, bf16[4,8,128,1,64]{2,4,1,3,0:T(8,128)(2,1)S(1)}, s32[4,...) while((s32[]{:T(128)}, f32[4,8,1,128]{3,1,2,0:T(8,128)S(1)}, ...), condition=%wide.region_3.4_spmd, body=%wide.region_0.3_spmd.sunk | while | flops 34601984 | bytes 2138309 | solution.py:61
  391.9 80.6 %all-to-all-done.3 = bf16[64,2,8192]{2,1,0:T(2,128)(2,1)} async-done(((bf16[64,2,8192]{2,1,0:T(2,128)(2,1)}), bf16[64,2,8192]{2,1,0:T(2,128)(2,1)}, u32[]{:S(2)}, u32[]{:S(2)}) %all-to-all-start.3) | async-done | bytes 2097184 | tf_op jit(solution)/shard_map/all_to_all | solution.py:128
  472.5 2.7 reshape.494
  475.2 2.2 gather_fusion.4
  477.5 3.3 concatenate.62
  480.7 3.5 multiply_reduce_fusion
  485.8 11.1 %scatter_custom_fusion = bf16[4096,64]{1,0:T(8,128)(2,1)S(1)} fusion(s32[4096]{0:T(1024)S(1)} %get-tuple-element.228, bf16[4096,64]{1,0:T(8,128)(2,1)S(1)} %fusion.45, bf16[]{:T(256)} %constant.68.clone.1), kind=kCustom, calls=%fused_computation.81 | custom fusion | bytes 524290 | tf_op jit(solution)/shard_map/scatter | solution.py:170
  497.3 20.6 %all_to_all.67 = bf16[8,512,64]{1,2,0:T(8,128)(2,1)S(1)} all-to-all(bf16[8,512,64]{1,2,0:T(8,128)(2,1)S(1)} %copy.167), channel_id=1, replica_groups=mesh['dom'=64,'head'=8] {'head'}, dimensions={0} | all-to-all | bytes 1048576 | tf_op jit(solution)/shard_map/all_to_all | solution.py:171
  519.0 16.2 %all-gather.5.cloned.1.call-done = bf16[1536,768]{1,0:T(8,128)(2,1)} async-done(((bf16[24,768]{1,0:T(8,128)(2,1)}), bf16[1536,768]{1,0:T(8,128)(2,1)}) %all-gather.5.cloned.1.call-update) | async-done | bytes 2359312 | tf_op jit(solution)/shard_map/all_gather | solution.py:185
  535.2 6.4 %fusion.73 = (f32[512]{0:T(512)S(1)}, f32[512,768]{1,0:T(8,128)}) fusion(bf16[1536,768]{1,0:T(8,128)(2,1)} %all-gather.5.cloned.1.call-done, bf16[768,1536]{0,1:T(8,128)(2,1)} %all-gather.3.cloned.1.call-done, f32[512,768]{1,0:T(8,128)S(1)} %get-tuple-element.230, f32[768]{0:T(1024)S(1)} %copy-done.12, f32[512]{0:T(512)S(1)} %add_rsqrt_fusion.1, ...), kind=kOutput, calls=%fused_computation.132 | convolution fusion | flops 2427321856 | bytes 7873536 | tf_op jit(solution)/shard_map/dot_general | solution.py:183
  541.6 1.8 multiply_reduce_fusion.1
  (200 shorter events, 67.0 us)
Async XLA Ops:
  6.5 511.4 %copy-start = (bf16[512,768]{1,0:T(8,128)(2,1)S(1)}, bf16[512,768]{1,0:T(8,128)(2,1)}, u32[]{:S(2)}) copy-start(bf16[512,768]{1,0:T(8,128)(2,1)} %param.17) | copy-start | bytes 2359300
  14.7 10.5 %copy-start.10 = (s32[32,2]{0,1:T(2,128)S(1)}, s32[32,2]{0,1:T(2,128)}, u32[]{:S(2)}) copy-start(s32[32,2]{0,1:T(2,128)} %param.23) | copy-start | bytes 772
  14.7 10.7 %copy-start.11 = (s32[32,2]{0,1:T(2,128)S(1)}, s32[32,2]{0,1:T(2,128)}, u32[]{:S(2)}) copy-start(s32[32,2]{0,1:T(2,128)} %param.24) | copy-start | bytes 772
  14.7 12.4 %copy-start.8 = (s32[4096]{0:T(1024)S(1)}, s32[4096]{0:T(1024)}, u32[]{:S(2)}) copy-start(s32[4096]{0:T(1024)} %param.22) | copy-start | bytes 49156
  14.7 36.9 %all-to-all-start = ((bf16[3,512,512]{1,0,2:T(4,128)(2,1)}), bf16[3,512,512]{1,0,2:T(4,128)(2,1)S(1)}, u32[]{:S(2)}, u32[]{:S(2)}) async-start(bf16[3,512,512]{1,0,2:T(4,128)(2,1)} %copy.139), calls=%async_computation | async-start | bytes 4194304 | tf_op jit(solution)/shard_map/all_to_all | solution.py:92
  51.6 84.9 %all-to-all-start.1 = ((s32[64,1,2]{2,1,0:T(1,128)}), s32[64,1,2]{2,1,0:T(1,128)S(1)}, u32[]{:S(2)}, u32[]{:S(2)}) async-start(s32[64,1,2]{2,1,0:T(1,128)} %bitcast.27), calls=%async_computation.1 | async-start | bytes 65536 | tf_op jit(solution)/shard_map/all_to_all | solution.py:118
  136.5 16.9 %copy-start.1 = (s32[32]{0:T(128)S(1)}, s32[32]{0:T(128)}, u32[]{:S(2)}) copy-start(s32[32]{0:T(128)} %param.25) | copy-start | bytes 388
  136.5 111.8 %all-to-all-start.2 = ((bf16[64,2,8192]{2,1,0:T(2,128)(2,1)}), bf16[64,2,8192]{2,1,0:T(2,128)(2,1)}, u32[]{:S(2)}, u32[]{:S(2)}) async-start(bf16[64,2,8192]{2,1,0:T(2,128)(2,1)} %reshape.491), calls=%async_computation.2 | async-start | bytes 4194304 | tf_op jit(solution)/shard_map/all_to_all | solution.py:117
  151.3 367.7 %all-gather.3.cloned.1.call-start = ((), (), s32[]{:S(2)}) async-start(), calls=%async_computation.7 | async-start | bytes 2396160 | tf_op jit(solution)/shard_map/all_gather | solution.py:179
  156.5 1.0 copy-start.2
  345.2 18.1 %all-to-all-start.4 = ((bf16[64,2,128]{2,1,0:T(2,128)(2,1)}), bf16[64,2,128]{2,1,0:T(2,128)(2,1)S(1)}, u32[]{:S(2)}, u32[]{:S(2)}) async-start(bf16[64,2,128]{2,1,0:T(2,128)(2,1)} %bitcast.37), calls=%async_computation.4 | async-start | bytes 65536 | tf_op jit(solution)/shard_map/all_to_all | solution.py:142
  362.4 16.0 %copy-start.3 = (bf16[1,4096,64]{2,1,0:T(8,128)(2,1)S(1)}, bf16[1,4096,64]{2,1,0:T(8,128)(2,1)}, u32[]{:S(2)}) copy-start(bf16[1,4096,64]{2,1,0:T(8,128)(2,1)} %copy-done.2) | copy-start | bytes 1572868
  362.4 16.5 %copy-start.4 = (bf16[1,4096,64]{2,1,0:T(8,128)(2,1)S(1)}, bf16[1,4096,64]{2,1,0:T(8,128)(2,1)}, u32[]{:S(2)}) copy-start(bf16[1,4096,64]{2,1,0:T(8,128)(2,1)} %copy.185) | copy-start | bytes 1572868
  363.2 109.2 %all-to-all-start.3 = ((bf16[64,2,8192]{2,1,0:T(2,128)(2,1)}), bf16[64,2,8192]{2,1,0:T(2,128)(2,1)}, u32[]{:S(2)}, u32[]{:S(2)}) async-start(bf16[64,2,8192]{2,1,0:T(2,128)(2,1)} %reshape_reshape.9), calls=%async_computation.3 | async-start | bytes 4194304 | tf_op jit(solution)/shard_map/all_to_all | solution.py:128
  377.4 157.8 %all-gather.5.cloned.1.call-start = ((), (), s32[]{:S(2)}) async-start(), calls=%async_computation.8 | async-start | bytes 2396160 | tf_op jit(solution)/shard_map/all_gather | solution.py:185
  380.0 2.2 copy-start.7
  497.0 21.0 %copy-start.6 = (bf16[512,768]{1,0:T(8,128)(2,1)S(1)}, bf16[512,768]{1,0:T(8,128)(2,1)}, u32[]{:S(2)}) copy-start(bf16[512,768]{1,0:T(8,128)(2,1)} %param.15) | copy-start | bytes 2359300
  517.9 17.2 %copy-start.12 = (f32[768]{0:T(1024)S(1)}, f32[768]{0:T(1024)}, u32[]{:S(2)}) copy-start(f32[768]{0:T(1024)} %param.18) | copy-start | bytes 9220
  519.0 24.4 %copy-start.9 = (f32[768]{0:T(1024)S(1)}, f32[768]{0:T(1024)}, u32[]{:S(2)}) copy-start(f32[768]{0:T(1024)} %param.21) | copy-start | bytes 9220
  541.6 1.9 copy-start.5
Sparse Core Ops, SparseCore 0:
  155.1 150.7 all-gather.2
  381.2 153.9 all-gather.4
where the time goes:
time: 561 us; the launch traced here: 551 us
  waiting for transfers between devices  206 us (37%)
  local copies, waits for them, and re-layouts  151 us (27%)
  matrix products  64.5 us (11%)
  starting transfers between devices  58.6 us (10%)
  blocking collectives  44.3 us (8%)
  between operations  13.8 us (2%)
  other arithmetic  13.3 us (2%)
    all_to_all x1, waiting for transfers between devices, per_device(): lax.all_to_all(outgoing, 'dom', split_axis=0, concat_axis=0, tiled=True)  82.9 us
    all_to_all x1, waiting for transfers between devices, per_device(): lax.all_to_all(shortened(partial_out.reshape(front_shape + (-1,))), 'dom'...  80.6 us
    dot_general x20, matrix products, attend_core(): jnp.einsum('phqk,pkhe->pqhe', weights.astype(jnp.bfloat16), value_blocks,...  33.1 us
    gather x1, local copies, waits for them, and re-layouts, per_device(): gathered[:, local_order, :].reshape(3, blocks, BLK, local_heads, HD)  30.6 us
    slice x1, local copies, waits for them, and re-layouts, per_device(): query_blocks = clustered[0]  28.1 us
    all_to_all x1, waiting for transfers between devices, per_device(): lax.all_to_all(projected, 'head', split_axis=2, concat_axis=1, tiled=True)  24.4 us
    all_to_all x1, blocking collectives, per_device(): lax.all_to_all(shortened(maxima.reshape(front_shape + (-1,))), 'dom', spl...  23.7 us
    dot_general x20, matrix products, attend_core(): jnp.einsum('pqhe,pkhe->phqk', query_blocks, key_blocks, preferred_element...  21.1 us
  transfers between devices with their start and end apart: 7, of which 5 were waited for; matrix products, arithmetic and copies ran while one was open for 38% of the time, Pallas kernels for 0%

commit v1 on v0

v1 whole, which is shorter than its diff:
```python
import functools

import jax
import jax.numpy as jnp
from jax import lax
from jax.experimental import pallas as pl
from jax.experimental.pallas import tpu as pltpu
from jax.sharding import PartitionSpec as P

HEADS = 8
HD = 64
BLK = 128
NZ = 16
NX = 4
PART = BLK // HEADS
HALF_RING = NZ // 2
FULL_HOPS = 4
MESH = pl.DeviceIdType.MESH
VMEM = pl.BlockSpec(memory_space=pltpu.VMEM)
SMEM = pl.BlockSpec(memory_space=pltpu.SMEM)
ANY = pl.BlockSpec(memory_space=pl.ANY)
LIMIT = 60 * 1024 * 1024


def greet(partners):
    barrier = pltpu.get_barrier_semaphore()
    for partner in partners:
        pl.semaphore_signal(barrier, inc=1, device_id=partner, device_id_type=MESH)
    pl.semaphore_wait(barrier, len(partners))


def send(source, target, send_sem, recv_sem, partner):
    copy = pltpu.make_async_remote_copy(
        src_ref=source,
        dst_ref=target,
        send_sem=send_sem,
        recv_sem=recv_sem,
        device_id=partner,
        device_id_type=MESH,
    )
    copy.start()
    return copy


def cluster_kernel(
    features,
    picked,
    extra,
    own_table,
    carried,
    tables,
    weights,
    pool,
    total,
    send_sem,
    recv_sem,
    table_send,
    table_recv,
    ring_send,
    ring_recv,
    local_sem,
):
    dom, head = lax.axis_index("dom"), lax.axis_index("head")
    z, x = dom // NX, lax.rem(dom, NX)
    y, core = head // 2, lax.rem(head, 2)

    def at(step, other):
        return lax.rem(y + step, 4) * 2 + lax.rem(core + other, 2)

    right, left, peer = {"head": at(1, 0)}, {"head": at(3, 0)}, {"head": at(0, 1)}
    planes = [None] + [{"dom": lax.rem(z + step, NZ) * NX + x} for step in range(1, NZ)]
    columns = [None] + [{"dom": z * NX + lax.rem(x + step, NX)} for step in range(1, NX)]
    greet([right, left, peer] + planes[1:] + columns[1:])
    started = []

    def put(*operands):
        started.append(send(*operands))
        return started[-1]

    rows = features.shape[0]
    half = rows // 2
    upper, lower = pl.ds(0, half), pl.ds(half, half)

    def go(number, source, slot, part, partner):
        target = pool.at[slot] if part is None else pool.at[slot, part]
        return put(source, target, send_sem.at[number], recv_sem.at[number], partner)

    def weights_go(direction, hop):
        place = HALF_RING * direction + hop
        return put(
            extra if hop == 1 else weights.at[place - 1],
            weights.at[place],
            ring_send.at[place],
            ring_recv.at[place],
            planes[1] if direction == 0 else planes[NZ - 1],
        )

    right_a = go(0, features.at[upper], 1, upper, right)
    left_b = go(1, features.at[lower], 2, lower, left)
    right_b = go(2, features.at[lower], 1, lower, right)
    left_a = go(3, features.at[upper], 2, upper, left)
    own_peer = go(4, features, 4, None, peer)
    hops = [weights_go(0, 1), weights_go(1, 1)]
    table_x = [
        put(own_table, tables.at[pl.ds(dom, 1)], table_send.at[step], table_recv.at[step], columns[step])
        for step in range(1, NX)
    ]
    own_weights = pltpu.make_async_copy(extra, weights.at[0], local_sem.at[0])
    own_weights.start()
    own_row = pltpu.make_async_copy(own_table, tables.at[pl.ds(dom, 1)], local_sem.at[1])
    own_row.start()

    row_ids = lax.broadcasted_iota(jnp.int32, (rows, rows), 1)
    wanted = picked[...]

    def add(block, owner, first=False):
        chosen = jnp.where(wanted - owner * rows == row_ids, 1.0, 0.0).astype(jnp.bfloat16)
        product = jnp.dot(chosen, block, preferred_element_type=jnp.float32)
        total[...] = product if first else total[...] + product

    def weights_on(hop):
        for direction in range(2):
            if hops[direction] is not None:
                hops[direction].wait_recv()
                last = hop == HALF_RING - direction
                hops[direction] = None if last else weights_go(direction, hop + 1)

    own_row.wait()
    for copy in table_x:
        copy.wait_recv()
    plane_rows = tables.at[pl.ds(z * NX, NX)]
    table_z = [
        put(plane_rows, plane_rows, table_send.at[NX + step], table_recv.at[NX + step], planes[step])
        for step in range(1, NZ)
    ]
    add(features[...], head, True)
    weights_on(1)
    right_a.wait_recv()
    on_a = go(5, pool.at[1, upper], 3, upper, right)
    left_b.wait_recv()
    on_b = go(6, pool.at[2, lower], 3, lower, left)
    weights_on(2)
    own_peer.wait_recv()
    add(pool[4], at(0, 1))
    weights_on(3)
    right_b.wait_recv()
    from_left = go(7, pool.at[1], 5, None, peer)
    left_a.wait_recv()
    from_right = go(8, pool.at[2], 6, None, peer)
    weights_on(4)
    add(pool[1], at(3, 0))
    weights_on(5)
    add(pool[2], at(1, 0))
    weights_on(6)
    from_left.wait_recv()
    add(pool[5], at(3, 1))
    weights_on(7)
    from_right.wait_recv()
    add(pool[6], at(1, 1))
    weights_on(8)
    on_a.wait_recv()
    on_b.wait_recv()
    across = go(9, pool.at[3], 7, None, peer)
    add(pool[3], at(2, 0))
    across.wait_recv()
    add(pool[7], at(2, 1))
    carried[...] = total[...].astype(jnp.bfloat16).reshape(rows // PART, PART, features.shape[1])
    for copy in table_z:
        copy.wait_recv()
    own_weights.wait()
    for copy in started:
        copy.wait_send()


def cluster(features, picked, extra, own_table):
    rows, width = features.shape
    dma = pltpu.SemaphoreType.DMA
    return pl.pallas_call(
        cluster_kernel,
        out_shape=(
            jax.ShapeDtypeStruct((rows // PART, PART, width), jnp.bfloat16),
            jax.ShapeDtypeStruct((NZ * NX,) + own_table.shape[1:], jnp.int32),
            jax.ShapeDtypeStruct((NZ,) + extra.shape, jnp.bfloat16),
        ),
        in_specs=[VMEM, VMEM, VMEM, VMEM],
        out_specs=(VMEM, VMEM, VMEM),
        scratch_shapes=[
            pltpu.VMEM((8, rows, width), jnp.bfloat16),
            pltpu.VMEM((rows, width), jnp.float32),
            dma((10,)),
            dma((10,)),
            dma((NX + NZ,)),
            dma((NX + NZ,)),
            dma((NZ,)),
            dma((NZ,)),
            dma((2,)),
        ],
        compiler_params=pltpu.CompilerParams(
            collective_id=1, has_side_effects=True, vmem_limit_bytes=LIMIT
        ),
        name="cluster_rows",
    )(features, picked, extra, own_table)


def hop_size(hop):
    return 32 if hop <= FULL_HOPS else 4 + 8 * (HALF_RING - hop)


def slot_base(step):
    return 0 if step == 0 else 8 + 16 * (step - 1)


def ring_kernel(
    wanted,
    carried,
    qkv_weight,
    weight_column,
    own_query,
    own_pair,
    slot_pair,
    weights,
    *scratch,
):
    full = scratch[: 2 * FULL_HOPS]
    ring_body(
        wanted,
        carried,
        qkv_weight,
        weight_column,
        own_query,
        own_pair,
        slot_pair,
        weights,
        full,
        *scratch[2 * FULL_HOPS :],
    )


def ring_body(
    wanted,
    carried,
    qkv_weight,
    weight_column,
    own_query,
    own_pair,
    slot_pair,
    weights,
    full,
    part_way,
    trimmed,
    picked,
    arrived,
    sent_own,
    sent_slot,
    ring_send,
    ring_recv,
    row_send,
    row_recv,
    spread_send,
    spread_recv,
    weight_send,
    weight_recv,
    own_send,
    own_recv,
    peer_send,
    peer_recv,
):
    dom, head = lax.axis_index("dom"), lax.axis_index("head")
    z, x = dom // NX, lax.rem(dom, NX)
    core = lax.rem(head, 2)
    width = carried.shape[2]

    def plane(step):
        return lax.rem(z + step + NZ, NZ)

    def column(step):
        return lax.rem(x + step, NX)

    up = {"dom": plane(1) * NX + x}
    down = {"dom": plane(-1) * NX + x}
    rows_x = [None] + [{"dom": z * NX + column(step)} for step in range(1, NX)]
    heads = [None] + [{"head": lax.rem(head + step, HEADS)} for step in range(1, HEADS)]
    peer = {"head": head + 1 - 2 * core}
    greet([up, down] + rows_x[1:] + heads[1:])
    started, locals_started = [], []

    def landing(direction, hop):
        if hop <= FULL_HOPS:
            return full[FULL_HOPS * direction + hop - 1]
        return part_way.at[direction, hop - FULL_HOPS - 1]

    def source_of(direction, hop):
        if hop == 1:
            return carried
        if hop == FULL_HOPS + 1:
            return trimmed.at[direction]
        return landing(direction, hop - 1)

    def parts_of(hop):
        size = hop_size(hop)
        if hop == HALF_RING:
            return [(0, size)]
        middle = size // 2
        return [(0, middle), (middle, size - middle)]

    def ring_go(direction, hop, part):
        first, count = parts_of(hop)[part]
        copy = send(
            source_of(direction, hop).at[pl.ds(first, count)],
            landing(direction, hop).at[pl.ds(first, count)],
            ring_send.at[direction, hop - 1, part],
            ring_recv.at[direction, hop - 1, part],
            up if direction == 0 else down,
        )
        started.append(copy)
        return copy

    def listed(plane_step, column_id, source, turn):
        return wanted[plane(plane_step) * NX + column_id, 0, 2 * source + turn]

    weight_copies = []

    def weights_along(step):
        if step:
            copy = send(
                weight_column,
                weights.at[core, NX - step],
                weight_send.at[step],
                weight_recv.at[step],
                rows_x[step],
            )
            started.append(copy)
        else:
            copy = pltpu.make_async_copy(weight_column, weights.at[core, 0], weight_send.at[0])
            copy.start()
        weight_copies.append(copy)

    slot_copies = {step: [] for step in range(HALF_RING + 1)}

    def slots_from_full(chunk, source, step, direction, buffer):
        base = slot_base(step) + 8 * direction
        for turn in range(2):
            arrived[base + turn] = chunk[listed(0, x, source, turn)]
        for along in range(1, NX):
            for turn in range(2):
                picked[buffer, along - 1, turn] = chunk[listed(0, column(along), source, turn)]
            copy = send(
                picked.at[buffer, along - 1],
                arrived.at[pl.ds(base + 2 * (NX - along), 2)],
                row_send.at[step, direction, along],
                row_recv.at[step, direction, along],
                rows_x[along],
            )
            started.append(copy)
            slot_copies[step].append(copy)

    def slots_from_trimmed(chunk, step, direction):
        if step == HALF_RING:
            first, count, base = 0, 1, slot_base(step) + direction
        else:
            first, count, base = 4 + 8 * (HALF_RING - 1 - step), 2, slot_base(step) + 8 * direction
        arrived[pl.ds(base, count)] = chunk[pl.ds(first + count * x, count)]
        for along in range(1, NX):
            copy = send(
                chunk.at[pl.ds(first + count * column(along), count)],
                arrived.at[pl.ds(base + 2 * (NX - along), count)],
                row_send.at[step, direction, along],
                row_recv.at[step, direction, along],
                rows_x[along],
            )
            started.append(copy)
            slot_copies[step].append(copy)

    def spread(source, target, number, send_sem, recv_sem, base, count):
        copies = []
        for step in range(1, HEADS):
            other = lax.rem(head + step, HEADS)
            copy = send(
                source.at[other, pl.ds(base, count)],
                target.at[pl.ds(base, count), head],
                send_sem.at[number, step],
                recv_sem.at[number, step],
                heads[step],
            )
            started.append(copy)
            copies.append(copy)
        copy = pltpu.make_async_copy(
            source.at[head, pl.ds(base, count)],
            target.at[pl.ds(base, count), head],
            send_sem.at[number, 0],
        )
        copy.start()
        locals_started.append(copy)
        return copies

    spread_copies = []

    def peer_weights():
        weight_copies[0].wait()
        for copy in weight_copies[1:]:
            copy.wait_recv()
        copy = send(weights.at[core], weights.at[core], peer_send, peer_recv, peer)
        started.append(copy)
        spread_copies.append(copy)

    lower_lanes = lax.broadcasted_iota(jnp.int32, (16 * PART, BLK), 1) < HD

    def store_pairs(rows, target, base):
        count = rows.shape[0] // PART
        width_all = HEADS * HD
        keys = jnp.dot(
            rows, qkv_weight[:, width_all : 2 * width_all], preferred_element_type=jnp.float32
        )
        values = jnp.dot(
            rows, qkv_weight[:, 2 * width_all :], preferred_element_type=jnp.float32
        )
        lower = lower_lanes[: rows.shape[0]]
        for pair in range(HEADS // 2):
            lanes = slice(pair * BLK, (pair + 1) * BLK)
            key, value = keys[:, lanes], values[:, lanes]
            even = jnp.where(lower, value, pltpu.roll(key, HD, 1))
            odd = jnp.where(lower, pltpu.roll(value, HD, 1), key)
            for other, tile in ((2 * pair, even), (2 * pair + 1, odd)):
                target[other, pl.ds(base, count)] = tile.astype(jnp.bfloat16).reshape(
                    count, PART, BLK
                )

    def store_queries(rows, target, base):
        count = rows.shape[0] // PART
        queries = jnp.dot(rows, qkv_weight[:, : HEADS * HD], preferred_element_type=jnp.float32)
        queries = queries * (HD**-0.5)
        lower = lower_lanes[: rows.shape[0]]
        for pair in range(HEADS // 2):
            query = queries[:, pair * BLK : (pair + 1) * BLK]
            even = jnp.where(lower, 0.0, pltpu.roll(query, HD, 1))
            odd = jnp.where(lower, 0.0, query)
            for other, tile in ((2 * pair, even), (2 * pair + 1, odd)):
                target[other, pl.ds(base, count)] = tile.astype(jnp.bfloat16).reshape(
                    count, PART, BLK
                )

    def project(step):
        count = 16 if 0 < step < HALF_RING else 8
        base = slot_base(step)
        for copy in slot_copies[step]:
            copy.wait_recv()
        rows = arrived[pl.ds(base, count)].reshape(count * PART, width)
        store_pairs(rows, sent_slot, base)
        spread_copies.extend(
            spread(sent_slot, slot_pair, step, spread_send, spread_recv, base, count)
        )

    ring = {}
    for part in range(2):
        for direction in range(2):
            ring[direction, 1, part] = ring_go(direction, 1, part)
    slots_from_full(carried, dom, 0, 0, 0)

    @pl.loop(0, 2)
    def _(half):
        rows = carried[pl.ds(16 * half, 16)].reshape(16 * PART, width)
        store_queries(rows, sent_own.at[0], 16 * half)
        store_pairs(rows, sent_own.at[1], 16 * half)

    spread_copies.extend(spread(sent_own.at[0], own_query, 0, own_send, own_recv, 0, 32))
    spread_copies.extend(spread(sent_own.at[1], own_pair, 1, own_send, own_recv, 0, 32))

    for hop in range(1, HALF_RING + 1):
        last = hop == HALF_RING
        sources = [plane(-hop) * NX + x, plane(hop) * NX + x]
        for direction in range(2):
            ring[direction, hop, 0].wait_recv()
            if not last and hop != FULL_HOPS:
                ring[direction, hop + 1, 0] = ring_go(direction, hop + 1, 0)
        if not last:
            project(hop - 1)
            for direction in range(2):
                ring[direction, hop, 1].wait_recv()
                if hop != FULL_HOPS:
                    if (direction, hop + 1, 1) not in ring and hop + 1 < HALF_RING:
                        ring[direction, hop + 1, 1] = ring_go(direction, hop + 1, 1)
        if hop == FULL_HOPS:
            for direction in range(2):
                sign = 1 if direction == 0 else -1
                chunk = landing(direction, hop)
                for column_id in range(NX):
                    trimmed[direction, column_id] = chunk[
                        listed(sign * (HALF_RING - hop), column_id, sources[direction], direction)
                    ]
                for ahead in range(HALF_RING - hop - 1, 0, -1):
                    first = 4 + 8 * (HALF_RING - hop - 1 - ahead)
                    for column_id in range(NX):
                        for turn in range(2):
                            trimmed[direction, first + 2 * column_id + turn] = chunk[
                                listed(sign * ahead, column_id, sources[direction], turn)
                            ]
                for part in range(2):
                    ring[direction, hop + 1, part] = ring_go(direction, hop + 1, part)
        for direction in range(2):
            chunk = landing(direction, hop)
            if hop <= FULL_HOPS:
                slots_from_full(
                    chunk, sources[direction], hop, direction, 1 + 2 * (hop - 1) + direction
                )
            else:
                slots_from_trimmed(chunk, hop, direction)
        if hop <= NX:
            weights_along(hop - 1)
        if hop == HALF_RING - 1:
            peer_weights()
    project(HALF_RING - 1)
    project(HALF_RING)
    for copy in spread_copies:
        copy.wait_recv()
    for copy in started:
        copy.wait_send()
    for copy in locals_started:
        copy.wait()


def ring(wanted, carried, qkv_weight, weight_column):
    width = carried.shape[2]
    bf16 = jnp.bfloat16
    dma = pltpu.SemaphoreType.DMA
    return pl.pallas_call(
        ring_kernel,
        out_shape=(
            jax.ShapeDtypeStruct((32, HEADS, PART, BLK), bf16),
            jax.ShapeDtypeStruct((32, HEADS, PART, BLK), bf16),
            jax.ShapeDtypeStruct((128, HEADS, PART, BLK), bf16),
            jax.ShapeDtypeStruct((2, NX) + weight_column.shape, bf16),
        ),
        in_specs=[SMEM, VMEM, VMEM, VMEM],
        out_specs=(ANY, ANY, ANY, ANY),
        scratch_shapes=[pltpu.VMEM(carried.shape, bf16)] * (2 * FULL_HOPS)
        + [
            pltpu.VMEM((2, HALF_RING - FULL_HOPS, hop_size(FULL_HOPS + 1), PART, width), bf16),
            pltpu.VMEM((2, hop_size(FULL_HOPS + 1), PART, width), bf16),
            pltpu.VMEM((1 + 2 * FULL_HOPS, NX - 1, 2, PART, width), bf16),
            pltpu.VMEM((128, PART, width), bf16),
            pltpu.VMEM((2, HEADS, 32, PART, BLK), bf16),
            pltpu.VMEM((HEADS, 128, PART, BLK), bf16),
            dma((2, HALF_RING, 2)),
            dma((2, HALF_RING, 2)),
            dma((HALF_RING + 1, 2, NX)),
            dma((HALF_RING + 1, 2, NX)),
            dma((HALF_RING + 1, HEADS)),
            dma((HALF_RING + 1, HEADS)),
            dma((NX,)),
            dma((NX,)),
            dma((2, HEADS)),
            dma((2, HEADS)),
            dma,
            dma,
        ],
        compiler_params=pltpu.CompilerParams(
            collective_id=2, has_side_effects=True, vmem_limit_bytes=LIMIT
        ),
        name="ring_blocks",
    )(wanted, carried, qkv_weight, weight_column)


def attend_kernel(slots, counts, order, query, own_pair, slot_pair, out, held, merged):
    key_ids = lax.broadcasted_iota(jnp.int32, (BLK, BLK), 1)
    row_ids = lax.broadcasted_iota(jnp.int32, (BLK, BLK), 0)

    def one(block, place):
        queries = query[block]
        pairs = [own_pair[block], slot_pair[slots[2 * block]], slot_pair[slots[2 * block + 1]]]
        scores = []
        for turn, pair in enumerate(pairs):
            score = lax.dot_general(
                queries, pair, (((1,), (1,)), ((), ())), preferred_element_type=jnp.float32
            )
            scores.append(jnp.where(key_ids < counts[3 * block + turn], score, -1e30))
        peak = jnp.max(jnp.maximum(jnp.maximum(scores[0], scores[1]), scores[2]), 1, keepdims=True)
        weights = [jnp.exp(score - peak) for score in scores]
        total = jnp.sum(weights[0] + weights[1] + weights[2], 1, keepdims=True)
        summed = sum(
            jnp.dot(weight.astype(jnp.bfloat16), pair, preferred_element_type=jnp.float32)
            for weight, pair in zip(weights, pairs)
        )
        merged[place] = jnp.where(row_ids < counts[3 * block], summed / total, 0.0)

    @pl.loop(0, 16)
    def _(step):
        one(2 * step, 0)
        one(2 * step + 1, 1)

        @pl.loop(0, 16)
        def _(piece):
            for place in range(2):
                rows = merged[place, pl.ds(pl.multiple_of(8 * piece, 8), 8)]
                for row in range(8):
                    target = order[256 * step + 128 * place + 8 * piece + row]
                    held[pl.ds(target, 1), :] = rows[row : row + 1, :]

    out[...] = held[:, :HD].astype(jnp.bfloat16)


def attend(slots, counts, order, query, own_pair, slot_pair):
    rows = order.shape[0]
    return pl.pallas_call(
        attend_kernel,
        out_shape=jax.ShapeDtypeStruct((rows, HD), jnp.bfloat16),
        in_specs=[SMEM, SMEM, SMEM, VMEM, VMEM, VMEM],
        out_specs=VMEM,
        scratch_shapes=[
            pltpu.VMEM((rows, BLK), jnp.float32),
            pltpu.VMEM((2, BLK, BLK), jnp.float32),
        ],
        compiler_params=pltpu.CompilerParams(vmem_limit_bytes=LIMIT),
        name="attend_blocks",
    )(slots, counts, order, query, own_pair, slot_pair)


def regroup_kernel(attended, grouped, send_sem, recv_sem, local_sem):
    head = lax.axis_index("head")
    others = [lax.rem(head + step, HEADS) for step in range(1, HEADS)]
    greet([{"head": other} for other in others])
    copies = []
    for step, other in enumerate(others):
        copies.append(
            send(
                attended.at[other],
                grouped.at[head],
                send_sem.at[step],
                recv_sem.at[step],
                {"head": other},
            )
        )
    own = pltpu.make_async_copy(attended.at[head], grouped.at[head], local_sem)
    own.start()
    own.wait()
    for copy in copies:
        copy.wait()


def regroup(attended):
    return pl.pallas_call(
        regroup_kernel,
        out_shape=jax.ShapeDtypeStruct(attended.shape, attended.dtype),
        in_specs=[VMEM],
        out_specs=VMEM,
        scratch_shapes=[
            pltpu.SemaphoreType.DMA((HEADS - 1,)),
            pltpu.SemaphoreType.DMA((HEADS - 1,)),
            pltpu.SemaphoreType.DMA,
        ],
        compiler_params=pltpu.CompilerParams(
            collective_id=3, has_side_effects=True, vmem_limit_bytes=LIMIT
        ),
        name="regroup_heads",
    )(attended)


def layer_norm(values, gain):
    centered = values - jnp.mean(values, -1, keepdims=True)
    spread = jnp.mean(centered * centered, -1, keepdims=True)
    return centered * lax.rsqrt(spread + 1e-05) * gain


def tail_kernel(features, grouped, out_weight, attn_gain, weights, final_gain, out, mixed):
    attention = jnp.dot(grouped[0], out_weight[0], preferred_element_type=jnp.float32)
    for head in range(1, HEADS):
        attention += jnp.dot(grouped[head], out_weight[head], preferred_element_type=jnp.float32)
    residual_sum = features[...].astype(jnp.float32) + attention
    hidden_norm = layer_norm(residual_sum, attn_gain[...]).astype(jnp.bfloat16)
    mixed[...] = hidden_norm.astype(jnp.float32)
    tile = 512

    @pl.loop(0, weights.shape[1] // tile)
    def _(step):
        units = pl.ds(pl.multiple_of(step * tile, tile), tile)
        hidden = lax.dot_general(
            hidden_norm,
            weights[0, units],
            (((1,), (1,)), ((), ())),
            preferred_element_type=jnp.float32,
        )
        hidden = jax.nn.gelu(hidden).astype(jnp.bfloat16)
        mixed[...] += jnp.dot(hidden, weights[1, units], preferred_element_type=jnp.float32)

    out[...] = layer_norm(mixed[...], final_gain[...]).astype(jnp.bfloat16)


def tail(features, grouped, out_weight, attn_gain, weights, final_gain):
    return pl.pallas_call(
        tail_kernel,
        out_shape=jax.ShapeDtypeStruct(features.shape, jnp.bfloat16),
        in_specs=[VMEM] * 6,
        out_specs=VMEM,
        scratch_shapes=[pltpu.VMEM(features.shape, jnp.float32)],
        compiler_params=pltpu.CompilerParams(vmem_limit_bytes=LIMIT),
        name="tail_rows",
    )(features, grouped, out_weight, attn_gain, weights, final_gain)


def per_device(
    features,
    qkv_weight,
    out_weight,
    attn_gain,
    up_weight,
    down_weight,
    final_gain,
    node_order,
    dest_part,
    key_block,
    row_count,
):
    blocks, listed = dest_part.shape
    partitions = NZ * NX
    width = features.shape[1]
    dom, head = lax.axis_index("dom"), lax.axis_index("head")
    core = head % 2
    bf16 = jnp.bfloat16

    dest_flat, block_flat = dest_part.reshape(-1), key_block.reshape(-1)
    names = dest_flat[:, None] == jnp.arange(partitions, dtype=jnp.int32)[None, :]
    earlier = jnp.tril(dest_flat[:, None] == dest_flat[None, :], -1)
    turn = jnp.sum(earlier.astype(jnp.int32), 1)
    chosen = names[:, :, None] & (turn[:, None, None] == jnp.arange(2, dtype=jnp.int32))
    wanted = jnp.sum(jnp.where(chosen, block_flat[:, None, None], 0), 0).reshape(1, -1)
    own_table = jnp.stack([wanted[0], jnp.pad(row_count, (0, wanted.shape[1] - blocks))])[None]

    npart = node_order.shape[0]
    local_order = node_order - dom * npart
    picked = lax.dynamic_index_in_dim(
        local_order.reshape(blocks, HEADS, PART), head, 1, keepdims=False
    ).reshape(-1, 1)
    extra = jnp.where(core == 0, up_weight.T, down_weight)
    extra = jnp.pad(extra, ((0, 2 * PART - extra.shape[0]), (0, 0))).reshape(2, PART, width)
    carried, tables, weight_column = cluster(features, picked, extra, own_table)
    own_query, own_pair, slot_pair, weights = ring(tables, carried, qkv_weight, weight_column)

    z, x = dom // NX, dom % NX
    gap = (z - dest_flat // NX) % NZ
    across = (dest_flat % NX - x) % NX
    start = jnp.where(
        gap == 0,
        0,
        jnp.where(gap <= HALF_RING, 8 + 16 * (gap - 1), 8 + 16 * (NZ - gap - 1) + 8),
    )
    slots = start + 2 * across + turn
    listed_rows = tables[:, 1, :blocks].reshape(-1)[dest_flat * blocks + block_flat]
    counts = jnp.concatenate([row_count[:, None], listed_rows.reshape(blocks, listed)], 1)

    attended = attend(
        slots,
        counts.reshape(-1),
        local_order,
        own_query.reshape(blocks, BLK, BLK),
        own_pair.reshape(blocks, BLK, BLK),
        slot_pair.reshape(2 * partitions, BLK, BLK),
    )
    grouped = regroup(attended.reshape(HEADS, npart // HEADS, HD))
    return tail(
        features,
        grouped,
        out_weight.reshape(HEADS, HD, width),
        attn_gain.reshape(1, width),
        weights.reshape(2, partitions * 2 * PART, width),
        final_gain.reshape(1, width),
    )


def solution(mesh):
    in_specs = (
        P(("dom", "head"), None),
        P(),
        P(),
        P(),
        P(None, "dom"),
        P("dom", None),
        P(),
        P("dom"),
        P("dom", None),
        P("dom", None),
        P("dom"),
    )
    out_specs = P(("dom", "head"), None)
    return jax.shard_map(
        per_device, mesh=mesh, in_specs=in_specs, out_specs=out_specs, check_vma=False
    )
```

time: 561 us -> 254 us (0.45); the launches traced: 551 us -> 254 us
  Pallas kernels: 0 us -> 241 us
  waiting for transfers between devices: 206 us -> 0 us
  local copies, waits for them, and re-layouts: 151 us -> 8.89 us
  matrix products: 64.5 us -> 0 us
  starting transfers between devices: 58.6 us -> 0 us
  blocking collectives: 44.3 us -> 0 us
  between operations: 13.8 us -> 0.16 us
  other arithmetic: 13.3 us -> 3.8 us
    pallas_call x0 -> x5, Pallas kernels: none -> 241 us  [the longest x1 135 us: ring(): pl.pallas_call(ring_kernel, out_shape=(jax.ShapeDtypeStruct((32, HEADS, P...]
    all_to_all x5 -> x0, waiting for transfers between devices: 189 us -> none  [the longest x1 82.9 us: per_device(): lax.all_to_all(outgoing, 'dom', split_axis=0, concat_axis=0, tiled=True)]
    dot_general x44 -> x0, matrix products: 64.5 us -> none  [the longest x20 33.1 us: attend_core(): jnp.einsum('phqk,pkhe->pqhe', weights.astype(jnp.bfloat16), value_blocks,...]
    all_to_all x5 -> x0, starting transfers between devices: 58 us -> none  [the longest x1 14.8 us: per_device(): lax.all_to_all(outgoing, 'dom', split_axis=0, concat_axis=0, tiled=True)]
    all_to_all x2 -> x0, blocking collectives: 44.3 us -> none  [the longest x1 23.7 us: per_device(): lax.all_to_all(shortened(maxima.reshape(front_shape + (-1,))), 'dom', spl...]
    gather x7 -> x1, local copies, waits for them, and re-layouts: 38.4 us -> 0.77 us  [per_device(): tables[:, 1, :blocks].reshape(-1)[dest_flat * blocks + block_flat]]
    slice x1, local copies, waits for them, and re-layouts: 28.1 us -> 0.94 us  [per_device(): tables[:, 1, :blocks].reshape(-1)[dest_flat * blocks + block_flat]]
    all_gather x2 -> x0, waiting for transfers between devices: 16.2 us -> none  [the longest x1 16.2 us: per_device(): lax.all_gather(down_weight, 'dom', axis=0, tiled=True)]
  transfers between devices with their start and end apart: 7 -> 0, of which waited for: 5 -> 0; matrix products, arithmetic and copies ran while one was open for 38% -> 0% of each run, Pallas kernels for 0% -> 0%
where the time goes in v1:
time: 254 us
  Pallas kernels  241 us (95%)
  local copies, waits for them, and re-layouts  8.89 us (4%)
  other arithmetic  3.8 us (1%)
    pallas_call x1, Pallas kernels, ring(): pl.pallas_call(ring_kernel, out_shape=(jax.ShapeDtypeStruct((32, HEADS, P...  135 us
    pallas_call x1, Pallas kernels, cluster(): pl.pallas_call(cluster_kernel, out_shape=(jax.ShapeDtypeStruct((rows // P...  54.6 us
    pallas_call x1, Pallas kernels, attend(): pl.pallas_call(attend_kernel, out_shape=jax.ShapeDtypeStruct((rows, HD),...  20.6 us
    pallas_call x1, Pallas kernels, regroup(): pl.pallas_call(regroup_kernel, out_shape=jax.ShapeDtypeStruct(attended.sh...  18.5 us
    pallas_call x1, Pallas kernels, tail(): pl.pallas_call(tail_kernel, out_shape=jax.ShapeDtypeStruct(features.shape...  11.9 us

profile of v1, /device:TPU:1, one launch (start us, length us, event | category | flops | bytes accessed | tf_op | source)
XLA Modules:
  0.0 253.8 jit_solution(9896428066146023590)
XLA Ops:
  0.0 0.8 copy.27
  0.8 0.1 reshape.123
  0.9 0.2 convert_reduce_fusion
  1.1 0.5 fusion.2.slots
  1.6 0.7 broadcast_subtract_fusion.order
  2.3 0.0 copy-start
  2.3 0.1 reshape.124
  2.4 0.1 dynamic-slice_reduce_fusion
  2.5 0.9 reshape.145.picked
  3.4 0.8 bitcast_select_fusion
  4.2 0.6 pad.8
  4.8 0.7 pad_bitcast_fusion
  5.4 0.8 copy.28
  6.2 0.1 broadcast_in_dim.33
  6.3 0.1 iota_compare_fusion
  6.4 0.1 select_reduce_fusion
  6.5 0.1 copy.29
  6.6 0.1 stack_squeeze_reshape.3
  6.8 0.6 add_bitcast_fusion.own_table
  7.3 54.6 %cluster_rows.1 = (bf16[32,16,768]{2,1,0:T(8,128)(2,1)}, s32[64,2,128]{2,1,0:T(2,128)}, bf16[16,2,16,768]{3,2,1,0:T(8,128)(2,1)}) custom-call(bf16[512,768]{1,0:T(8,128)(2,1)} %features.3, s32[512,1]{1,0:T(8,128)} %reshape.145.picked, bf16[2,16,768]{2,1,0:T(8,128)(2,1)} %bitcast.22, s32[1,2,128]{2,1,0:T(2,128)} %add_bitcast_fusion.own_table), custom_call_target="tpu_custom_call" | custom-call | tf_op jit(solution)/shard_map/cluster_rows/pallas_call | solution.py:178
  62.0 0.9 slice_reduce_fusion
  62.9 0.1 reshape_squeeze.3
  63.0 0.7 multiply_add_fusion
  63.7 0.1 copy.31
  63.8 0.1 add.94
  63.9 0.8 gather_fusion
  64.7 0.1 reshape.127
  64.8 0.7 copy.32
  65.6 0.1 pad_add_fusion
  65.6 0.6 reshape.128.counts
  66.3 135.3 %ring_blocks.1 = (bf16[32,8,16,128]{3,2,1,0:T(8,128)(2,1)}, bf16[32,8,16,128]{3,2,1,0:T(8,128)(2,1)}, bf16[128,8,16,128]{3,2,1,0:T(8,128)(2,1)}, bf16[2,4,16,2,16,768]{5,4,3,2,1,0:T(8,128)(2,1)}) custom-call(s32[64,2,128]{2,1,0:T(2,128)} %get-tuple-element.12.wanted, bf16[32,16,768]{2,1,0:T(8,128)(2,1)} %get-tuple-element.13.carried, ...), custom_call_target="tpu_custom_call" | custom-call | tf_op jit(solution)/shard_map/ring_blocks/pallas_call | solution.py:525
  201.5 0.0 copy-done
  201.5 0.0 copy-start.1
  201.5 0.0 copy-start.2
  201.5 20.6 %attend_blocks.1 = bf16[4096,64]{1,0:T(8,128)(2,1)} custom-call(s32[64]{0:T(128)} %fusion.2.slots, s32[96]{0:T(128)} %reshape.128.counts, s32[4096]{0:T(1024)} %copy-done, bf16[32,128,128]{2,1,0:T(8,128)(2,1)} %bitcast.19, bf16[32,128,128]{2,1,0:T(8,128)(2,1)} %bitcast.20, bf16[128,128,128]{2,1,0:T(8,128)(2,1)} %bitcast.17), custom_call_target="tpu_custom_call" | custom-call | tf_op jit(solution)/shard_map/attend_blocks/pallas_call | solution.py:603
  222.2 18.5 %regroup_heads.1.grouped = bf16[8,512,64]{2,1,0:T(8,128)(2,1)} custom-call(bf16[8,512,64]{2,1,0:T(8,128)(2,1)} %bitcast.18), custom_call_target="tpu_custom_call" | custom-call | tf_op jit(solution)/shard_map/regroup_heads/pallas_call | solution.py:640
  240.7 0.0 copy-done.1
  240.7 0.6 reshape.134.attn_gain
  241.3 0.0 copy-done.2
  241.3 0.6 reshape.136.final_gain
  241.8 11.9 %tail_rows.1 = bf16[512,768]{1,0:T(8,128)(2,1)} custom-call(bf16[512,768]{1,0:T(8,128)(2,1)} %features.3, bf16[8,512,64]{2,1,0:T(8,128)(2,1)} %regroup_heads.1.grouped, bf16[8,64,768]{2,1,0:T(8,128)(2,1)} %bitcast.21, f32[1,768]{1,0:T(1,128)} %reshape.134.attn_gain, bf16[2,2048,768]{2,1,0:T(8,128)(2,1)} %bitcast.16, f32[1,768]{1,0:T(1,128)} %reshape.136.final_gain), custom_call_target="tpu_custom_call" | custom-call | tf_op jit(solution)/shard_map/tail_rows/pallas_call | solution.py:688
  (4 shorter events, 0.0 us)
Async XLA Ops:
  2.3 199.2 %copy-start = (s32[4096]{0:T(1024)}, s32[4096]{0:T(1024)S(1)}, u32[]{:S(2)}) copy-start(s32[4096]{0:T(1024)S(1)} %broadcast_subtract_fusion.order) | copy-start | bytes 49156
  201.5 39.1 %copy-start.1 = (f32[768]{0:T(1024)S(1)}, f32[768]{0:T(1024)}, u32[]{:S(2)}) copy-start(f32[768]{0:T(1024)} %param.14) | copy-start | bytes 9220
  201.5 39.7 %copy-start.2 = (f32[768]{0:T(1024)S(1)}, f32[768]{0:T(1024)}, u32[]{:S(2)}) copy-start(f32[768]{0:T(1024)} %param.17) | copy-start | bytes 9220

commit v2 on v0

v2 whole, which is shorter than its diff:
```python
import functools

import jax
import jax.numpy as jnp
from jax import lax
from jax.experimental import pallas as pl
from jax.experimental.pallas import tpu as pltpu
from jax.sharding import PartitionSpec as P

HEADS = 8
HD = 64
BLK = 128
NZ = 16
NX = 4
PART = BLK // HEADS
HALF_RING = NZ // 2
FULL_HOPS = 4
MESH = pl.DeviceIdType.MESH
VMEM = pl.BlockSpec(memory_space=pltpu.VMEM)
SMEM = pl.BlockSpec(memory_space=pltpu.SMEM)
ANY = pl.BlockSpec(memory_space=pl.ANY)
LIMIT = 60 * 1024 * 1024


def greet(partners):
    barrier = pltpu.get_barrier_semaphore()
    for partner in partners:
        pl.semaphore_signal(barrier, inc=1, device_id=partner, device_id_type=MESH)
    pl.semaphore_wait(barrier, len(partners))


def send(source, target, send_sem, recv_sem, partner):
    copy = pltpu.make_async_remote_copy(
        src_ref=source,
        dst_ref=target,
        send_sem=send_sem,
        recv_sem=recv_sem,
        device_id=partner,
        device_id_type=MESH,
    )
    copy.start()
    return copy


def hop_size(hop):
    return 32 if hop <= FULL_HOPS else 4 + 8 * (HALF_RING - hop)


def slot_base(step):
    return 0 if step == 0 else 8 + 16 * (step - 1)


def exchange_kernel(*refs):
    inputs, outputs, scratch = refs[:7], refs[7:12], refs[12:]
    whole = 4 * FULL_HOPS + 2
    exchange_body(*inputs, *outputs, scratch[:2], scratch[2:whole], *scratch[whole:])


def exchange_body(
    features,
    picked,
    up_rows,
    down_rows,
    wanted_row,
    count_row,
    qkv_weight,
    own_query,
    own_pair,
    slot_pair,
    weights,
    tables,
    carried,
    full,
    pool,
    total,
    extra,
    own_table,
    weight_column,
    wanted,
    part_way,
    trimmed,
    chosen,
    arrived,
    sent_own,
    sent_slot,
    pool_send,
    pool_recv,
    table_send,
    table_recv,
    column_send,
    column_recv,
    ring_send,
    ring_recv,
    row_send,
    row_recv,
    spread_send,
    spread_recv,
    weight_send,
    weight_recv,
    own_send,
    own_recv,
    peer_send,
    peer_recv,
    local_sem,
):
    dom, head = lax.axis_index("dom"), lax.axis_index("head")
    z, x = dom // NX, lax.rem(dom, NX)
    y, core = head // 2, lax.rem(head, 2)
    rows, width = features.shape
    part_width = width // 2

    def plane(step):
        return lax.rem(z + step + NZ, NZ)

    def column(step):
        return lax.rem(x + step, NX)

    def at(step, other):
        return lax.rem(y + step, 4) * 2 + lax.rem(core + other, 2)

    planes = [None] + [{"dom": plane(step) * NX + x} for step in range(1, NZ)]
    rows_x = [None] + [{"dom": z * NX + column(step)} for step in range(1, NX)]
    heads = [None] + [{"head": lax.rem(head + step, HEADS)} for step in range(1, HEADS)]
    right, left, peer = {"head": at(1, 0)}, {"head": at(3, 0)}, {"head": at(0, 1)}
    up, down = planes[1], planes[NZ - 1]
    greet(planes[1:] + rows_x[1:] + heads[1:])
    started, locals_started = [], []

    def put(*operands):
        started.append(send(*operands))
        return started[-1]

    def local(source, target, number):
        copy = pltpu.make_async_copy(source, target, local_sem.at[number])
        copy.start()
        return copy

    half = rows // 2
    upper, lower = pl.ds(0, half), pl.ds(half, half)

    def pool_go(part, number, source, slot, which, partner):
        target = pool.at[part, slot] if which is None else pool.at[part, slot, which]
        return put(source, target, pool_send.at[part, number], pool_recv.at[part, number], partner)

    def pool_own(part):
        lanes = pl.ds(part * part_width, part_width)
        return {
            "right_a": pool_go(part, 0, features.at[upper, lanes], 1, upper, right),
            "left_b": pool_go(part, 1, features.at[lower, lanes], 2, lower, left),
            "right_b": pool_go(part, 2, features.at[lower, lanes], 1, lower, right),
            "left_a": pool_go(part, 3, features.at[upper, lanes], 2, upper, left),
            "own_peer": pool_go(part, 4, features.at[:, lanes], 4, None, peer),
        }

    def weights_go(direction, hop):
        place = HALF_RING * direction + hop
        return put(
            extra if hop == 1 else weight_column.at[place - 1],
            weight_column.at[place],
            column_send.at[place],
            column_recv.at[place],
            up if direction == 0 else down,
        )

    first_pool = pool_own(0)
    own_table[0, :, : wanted_row.shape[1]] = wanted_row[...]
    own_table[0, :, wanted_row.shape[1] :] = count_row[...]
    table_x = [
        put(own_table, tables.at[pl.ds(dom, 1)], table_send.at[step], table_recv.at[step], rows_x[step])
        for step in range(1, NX)
    ]
    own_row = local(own_table, tables.at[pl.ds(dom, 1)], 0)
    units = jnp.where(core == 0, up_rows[...], down_rows[...])
    filler = jnp.zeros((2 * PART - units.shape[0], width), units.dtype)
    extra[...] = jnp.concatenate([units, filler], 0).reshape(2, PART, width)
    hops = [weights_go(0, 1), weights_go(1, 1)]
    own_weights = local(extra, weight_column.at[0], 1)

    def weights_on(hop):
        for direction in range(2):
            if hops[direction] is not None:
                hops[direction].wait_recv()
                last = hop == HALF_RING - direction
                hops[direction] = None if last else weights_go(direction, hop + 1)

    row_ids = lax.broadcasted_iota(jnp.int32, (rows, rows), 1)
    picks = picked[...]

    def add(block, owner, first=False):
        hit = jnp.where(picks - owner * rows == row_ids, 1.0, 0.0).astype(jnp.bfloat16)
        product = jnp.dot(hit, block, preferred_element_type=jnp.float32)
        total[...] = product if first else total[...] + product

    def gather_rows(part, got, along):
        add(features[:, part * part_width : (part + 1) * part_width], head, True)
        got["right_a"].wait_recv()
        on_a = pool_go(part, 5, pool.at[part, 1, upper], 3, upper, right)
        got["left_b"].wait_recv()
        on_b = pool_go(part, 6, pool.at[part, 2, lower], 3, lower, left)
        along(0)
        got["own_peer"].wait_recv()
        add(pool[part, 4], at(0, 1))
        along(1)
        got["right_b"].wait_recv()
        from_left = pool_go(part, 7, pool.at[part, 1], 5, None, peer)
        got["left_a"].wait_recv()
        from_right = pool_go(part, 8, pool.at[part, 2], 6, None, peer)
        along(2)
        add(pool[part, 1], at(3, 0))
        along(3)
        add(pool[part, 2], at(1, 0))
        along(4)
        from_left.wait_recv()
        add(pool[part, 5], at(3, 1))
        along(5)
        from_right.wait_recv()
        add(pool[part, 6], at(1, 1))
        along(6)
        on_a.wait_recv()
        on_b.wait_recv()
        across = pool_go(part, 9, pool.at[part, 3], 7, None, peer)
        add(pool[part, 3], at(2, 0))
        along(7)
        across.wait_recv()
        add(pool[part, 7], at(2, 1))
        carried[part][...] = (
            total[...].astype(jnp.bfloat16).reshape(rows // PART, PART, part_width)
        )

    def landing(direction, hop, part):
        if hop <= FULL_HOPS:
            return full[4 * (hop - 1) + 2 * direction + part]
        return part_way.at[direction, hop - FULL_HOPS - 1, part]

    def ring_go(direction, hop, part):
        if hop == 1:
            source = carried[part]
        elif hop == FULL_HOPS + 1:
            source = trimmed.at[direction, part]
        else:
            source = landing(direction, hop - 1, part)
        count = pl.ds(0, hop_size(hop))
        ring[direction, hop, part] = put(
            source.at[count],
            landing(direction, hop, part).at[count],
            ring_send.at[direction, hop - 1, part],
            ring_recv.at[direction, hop - 1, part],
            up if direction == 0 else down,
        )

    def listed(plane_step, column_id, source, turn):
        return wanted[plane(plane_step) * NX + column_id, 0, 2 * source + turn]

    def trim(direction, part):
        chunk = landing(direction, FULL_HOPS, part)
        sign = 1 if direction == 0 else -1
        source = plane(-sign * FULL_HOPS) * NX + x
        beyond = HALF_RING - FULL_HOPS
        for column_id in range(NX):
            trimmed[direction, part, column_id] = chunk[
                listed(sign * beyond, column_id, source, direction)
            ]
        for ahead in range(beyond - 1, 0, -1):
            first = 4 + 8 * (beyond - 1 - ahead)
            for column_id in range(NX):
                for turn in range(2):
                    trimmed[direction, part, first + 2 * column_id + turn] = chunk[
                        listed(sign * ahead, column_id, source, turn)
                    ]

    slot_copies = {step: [] for step in range(HALF_RING + 1)}

    def slot_go(source, base, step, direction, part, along, count):
        slot_copies[step].append(
            put(
                source,
                arrived.at[part, pl.ds(base + 2 * (NX - along), count)],
                row_send.at[step, direction, part, along],
                row_recv.at[step, direction, part, along],
                rows_x[along],
            )
        )

    def slots_along(step, direction, part):
        base = slot_base(step) + 8 * direction
        if step <= FULL_HOPS:
            chunk = landing(direction, step, part) if step else carried[part]
            source = plane(-step if direction == 0 else step) * NX + x
            buffer = 2 * step - 1 + direction if step else 0
            for turn in range(2):
                arrived[part, base + turn] = chunk[listed(0, x, source, turn)]
            for along in range(1, NX):
                for turn in range(2):
                    chosen[buffer, part, along - 1, turn] = chunk[
                        listed(0, column(along), source, turn)
                    ]
                slot_go(chosen.at[buffer, part, along - 1], base, step, direction, part, along, 2)
            return
        chunk = landing(direction, step, part)
        if step == HALF_RING:
            first, count, base = 0, 1, slot_base(step) + direction
        else:
            first, count = 4 + 8 * (HALF_RING - 1 - step), 2
        arrived[part, pl.ds(base, count)] = chunk[pl.ds(first + count * x, count)]
        for along in range(1, NX):
            source = chunk.at[pl.ds(first + count * column(along), count)]
            slot_go(source, base, step, direction, part, along, count)

    weight_copies, spread_copies = [], []

    def weights_along(step):
        if step:
            weight_copies.append(
                put(
                    weight_column,
                    weights.at[core, NX - step],
                    weight_send.at[step],
                    weight_recv.at[step],
                    rows_x[step],
                )
            )
        else:
            weight_copies.append(local(weight_column, weights.at[core, 0], 2))

    def peer_weights():
        weight_copies[0].wait()
        for copy in weight_copies[1:]:
            copy.wait_recv()
        spread_copies.append(put(weights.at[core], weights.at[core], peer_send, peer_recv, peer))

    def spread(source, target, number, send_sem, recv_sem, base, count):
        for step in range(1, HEADS):
            other = lax.rem(head + step, HEADS)
            spread_copies.append(
                put(
                    source.at[other, pl.ds(base, count)],
                    target.at[pl.ds(base, count), head],
                    send_sem.at[number, step],
                    recv_sem.at[number, step],
                    heads[step],
                )
            )
        copy = pltpu.make_async_copy(
            source.at[head, pl.ds(base, count)],
            target.at[pl.ds(base, count), head],
            send_sem.at[number, 0],
        )
        copy.start()
        locals_started.append(copy)

    lower_lanes = lax.broadcasted_iota(jnp.int32, (16 * PART, BLK), 1) < HD

    def store_tile(tile, target, other, base):
        count = tile.shape[0] // PART
        target[other, pl.ds(base, count)] = tile.astype(jnp.bfloat16).reshape(count, PART, BLK)

    def store_pairs(values_in, target, base):
        width_all = HEADS * HD
        keys = jnp.dot(
            values_in, qkv_weight[:, width_all : 2 * width_all], preferred_element_type=jnp.float32
        )
        values = jnp.dot(
            values_in, qkv_weight[:, 2 * width_all :], preferred_element_type=jnp.float32
        )
        is_lower = lower_lanes[: values_in.shape[0]]
        for pair in range(HEADS // 2):
            lanes = slice(pair * BLK, (pair + 1) * BLK)
            key, value = keys[:, lanes], values[:, lanes]
            even = jnp.where(is_lower, value, pltpu.roll(key, HD, 1))
            odd = jnp.where(is_lower, pltpu.roll(value, HD, 1), key)
            store_tile(even, target, 2 * pair, base)
            store_tile(odd, target, 2 * pair + 1, base)

    def store_queries(values_in, target, base):
        queries = jnp.dot(
            values_in, qkv_weight[:, : HEADS * HD], preferred_element_type=jnp.float32
        )
        queries = queries * (HD**-0.5)
        is_lower = lower_lanes[: values_in.shape[0]]
        for pair in range(HEADS // 2):
            query = queries[:, pair * BLK : (pair + 1) * BLK]
            store_tile(jnp.where(is_lower, 0.0, pltpu.roll(query, HD, 1)), target, 2 * pair, base)
            store_tile(jnp.where(is_lower, 0.0, query), target, 2 * pair + 1, base)

    def project_own():
        @pl.loop(0, 2)
        def _(step):
            blocks = pl.ds(16 * step, 16)
            joined = jnp.concatenate(
                [carried[part][blocks].reshape(16 * PART, part_width) for part in range(2)], 1
            )
            store_queries(joined, sent_own.at[0], 16 * step)
            store_pairs(joined, sent_own.at[1], 16 * step)

        spread(sent_own.at[0], own_query, 0, own_send, own_recv, 0, 32)
        spread(sent_own.at[1], own_pair, 1, own_send, own_recv, 0, 32)

    def project(step):
        count = 16 if 0 < step < HALF_RING else 8
        base = slot_base(step)
        for copy in slot_copies[step]:
            copy.wait_recv()
        joined = jnp.concatenate(
            [
                arrived[part, pl.ds(base, count)].reshape(count * PART, part_width)
                for part in range(2)
            ],
            1,
        )
        store_pairs(joined, sent_slot, base)
        spread(sent_slot, slot_pair, step, spread_send, spread_recv, base, count)

    ring, pools, table_z = {}, [first_pool], []

    def during_first(moment):
        if moment == 0:
            pools.append(pool_own(1))
            own_row.wait()
            for copy in table_x:
                copy.wait_recv()
            plane_rows = tables.at[pl.ds(z * NX, NX)]
            for step in range(1, NZ):
                table_z.append(
                    put(
                        plane_rows,
                        plane_rows,
                        table_send.at[NX + step],
                        table_recv.at[NX + step],
                        planes[step],
                    )
                )
        weights_on(moment + 1)

    gather_rows(0, pools[0], during_first)
    for direction in range(2):
        ring_go(direction, 1, 0)
    for copy in table_z:
        copy.wait_recv()
    local(tables, wanted, 3).wait()
    slots_along(0, 0, 0)
    gather_rows(1, pools[1], lambda moment: None)
    for direction in range(2):
        ring_go(direction, 1, 1)
    slots_along(0, 0, 1)
    own_weights.wait()

    for hop in range(1, HALF_RING + 1):
        for part in range(2):
            for direction in range(2):
                ring[direction, hop, part].wait_recv()
                if hop == FULL_HOPS:
                    trim(direction, part)
                if hop < HALF_RING:
                    ring_go(direction, hop + 1, part)
            for direction in range(2):
                slots_along(hop, direction, part)
            if hop == 1 and part == 0:
                project_own()
        if hop <= NX:
            weights_along(hop - 1)
        if hop == HALF_RING - 1:
            peer_weights()
        project(hop - 1)
    project(HALF_RING)
    for copy in spread_copies:
        copy.wait_recv()
    for copy in started:
        copy.wait_send()
    for copy in locals_started:
        copy.wait()


def exchange(features, picked, up_rows, down_rows, wanted_row, count_row, qkv_weight):
    rows, width = features.shape
    blocks, part_width = rows // PART, width // 2
    bf16 = jnp.bfloat16
    dma = pltpu.SemaphoreType.DMA
    tables = (NZ * NX, 1, 2 * wanted_row.shape[1])
    return pl.pallas_call(
        exchange_kernel,
        out_shape=(
            jax.ShapeDtypeStruct((blocks, HEADS, PART, BLK), bf16),
            jax.ShapeDtypeStruct((blocks, HEADS, PART, BLK), bf16),
            jax.ShapeDtypeStruct((2 * NZ * NX, HEADS, PART, BLK), bf16),
            jax.ShapeDtypeStruct((2, NX, NZ, 2, PART, width), bf16),
            jax.ShapeDtypeStruct(tables, jnp.int32),
        ),
        in_specs=[VMEM] * 7,
        out_specs=(ANY, ANY, ANY, ANY, ANY),
        scratch_shapes=[pltpu.VMEM((blocks, PART, part_width), bf16)] * (2 + 4 * FULL_HOPS)
        + [
            pltpu.VMEM((2, 8, rows, part_width), bf16),
            pltpu.VMEM((rows, part_width), jnp.float32),
            pltpu.VMEM((2, PART, width), bf16),
            pltpu.VMEM((1,) + tables[1:], jnp.int32),
            pltpu.VMEM((NZ, 2, PART, width), bf16),
            pltpu.SMEM(tables, jnp.int32),
            pltpu.VMEM(
                (2, HALF_RING - FULL_HOPS, 2, hop_size(FULL_HOPS + 1), PART, part_width), bf16
            ),
            pltpu.VMEM((2, 2, hop_size(FULL_HOPS + 1), PART, part_width), bf16),
            pltpu.VMEM((1 + 2 * FULL_HOPS, 2, NX - 1, 2, PART, part_width), bf16),
            pltpu.VMEM((2, 2 * NZ * NX, PART, part_width), bf16),
            pltpu.VMEM((2, HEADS, blocks, PART, BLK), bf16),
            pltpu.VMEM((HEADS, 2 * NZ * NX, PART, BLK), bf16),
            dma((2, 10)),
            dma((2, 10)),
            dma((NX + NZ,)),
            dma((NX + NZ,)),
            dma((NZ,)),
            dma((NZ,)),
            dma((2, HALF_RING, 2)),
            dma((2, HALF_RING, 2)),
            dma((HALF_RING + 1, 2, 2, NX)),
            dma((HALF_RING + 1, 2, 2, NX)),
            dma((HALF_RING + 1, HEADS)),
            dma((HALF_RING + 1, HEADS)),
            dma((NX,)),
            dma((NX,)),
            dma((2, HEADS)),
            dma((2, HEADS)),
            dma,
            dma,
            dma((4,)),
        ],
        compiler_params=pltpu.CompilerParams(
            collective_id=1, has_side_effects=True, vmem_limit_bytes=LIMIT
        ),
        name="exchange_blocks",
    )(features, picked, up_rows, down_rows, wanted_row, count_row, qkv_weight)


def attend_kernel(
    dest, key_block, turn, row_count, tables, order, query, own_pair, slot_pair, out, held, *merged
):
    key_ids = lax.broadcasted_iota(jnp.int32, (BLK, BLK), 1)
    row_ids = lax.broadcasted_iota(jnp.int32, (BLK, BLK), 0)
    dom = lax.axis_index("dom")
    z, x = dom // NX, lax.rem(dom, NX)
    node_base = dom * order.shape[0]

    def slot_of(entry):
        owner = dest[entry]
        gap = lax.rem(z - owner // NX + NZ, NZ)
        start = jnp.where(gap <= HALF_RING, 16 * gap - 8, 16 * (NZ - gap))
        start = jnp.where(gap == 0, 0, start)
        across = lax.rem(lax.rem(owner, NX) - x + NX, NX)
        return start + 2 * across + turn[entry], tables[owner, 0, 2 * NZ * NX + key_block[entry]]

    def one(block, target):
        queries = query[block]
        first, first_count = slot_of(2 * block)
        second, second_count = slot_of(2 * block + 1)
        own_count = row_count[block]
        pairs = [own_pair[block], slot_pair[first], slot_pair[second]]
        scores = []
        for pair, count in zip(pairs, (own_count, first_count, second_count)):
            score = lax.dot_general(
                queries, pair, (((1,), (1,)), ((), ())), preferred_element_type=jnp.float32
            )
            scores.append(jnp.where(key_ids < count, score, -1e30))
        peak = jnp.max(jnp.maximum(jnp.maximum(scores[0], scores[1]), scores[2]), 1, keepdims=True)
        weights = [jnp.exp(score - peak) for score in scores]
        total = jnp.sum(weights[0] + weights[1] + weights[2], 1, keepdims=True)
        summed = sum(
            jnp.dot(weight.astype(jnp.bfloat16), pair, preferred_element_type=jnp.float32)
            for weight, pair in zip(weights, pairs)
        )
        target[...] = jnp.where(row_ids < own_count, summed / total, 0.0)

    def place(block, source):
        for piece in range(BLK // 8):
            values = source[pl.ds(8 * piece, 8)]
            for row in range(8):
                node = order[BLK * block + 8 * piece + row] - node_base
                held[pl.ds(node, 1), :] = values[row : row + 1, :]

    blocks = query.shape[0]

    @pl.loop(0, blocks // 4)
    def _(step):
        for side in range(2):
            pair = 2 * step + side
            before = lax.rem(pair + blocks // 2 - 1, blocks // 2)
            for number in range(2):
                one(2 * pair + number, merged[2 * side + number])
                place(2 * before + number, merged[2 * (1 - side) + number])

    for number in range(2):
        place(blocks - 2 + number, merged[2 + number])
    half = BLK * blocks // HEADS // 2
    is_lower = lax.broadcasted_iota(jnp.int32, (half, BLK), 1) < HD
    for owner in range(HEADS):
        first = held[pl.ds(2 * half * owner, half)]
        second = held[pl.ds(2 * half * owner + half, half)]
        out[owner] = jnp.where(is_lower, first, pltpu.roll(second, HD, 1)).astype(jnp.bfloat16)


def attend(dest, key_block, turn, row_count, tables, order, query, own_pair, slot_pair):
    rows = order.shape[0]
    return pl.pallas_call(
        attend_kernel,
        out_shape=jax.ShapeDtypeStruct((HEADS, rows // HEADS // 2, BLK), jnp.bfloat16),
        in_specs=[SMEM] * 6 + [VMEM] * 3,
        out_specs=VMEM,
        scratch_shapes=[pltpu.VMEM((rows, BLK), jnp.float32)]
        + [pltpu.VMEM((BLK, BLK), jnp.float32)] * 4,
        compiler_params=pltpu.CompilerParams(vmem_limit_bytes=LIMIT),
        name="attend_blocks",
    )(dest, key_block, turn, row_count, tables, order, query, own_pair, slot_pair)


def layer_norm(values, gain):
    centered = values - jnp.mean(values, -1, keepdims=True)
    spread = jnp.mean(centered * centered, -1, keepdims=True)
    return centered * lax.rsqrt(spread + 1e-05) * gain


def finish_kernel(
    features,
    attended,
    out_weight,
    attn_gain,
    weights,
    final_gain,
    out,
    grouped,
    spaced,
    units,
    mixed,
    send_sem,
    recv_sem,
    local_sem,
):
    head = lax.axis_index("head")
    others = [lax.rem(head + step, HEADS) for step in range(1, HEADS)]
    greet([{"head": other} for other in others])
    copies = [
        send(
            attended.at[other], grouped.at[head], send_sem.at[step], recv_sem.at[step], {"head": other}
        )
        for step, other in enumerate(others)
    ]
    own = pltpu.make_async_copy(attended.at[head], grouped.at[head], local_sem.at[0])
    own.start()
    load = pltpu.make_async_copy(weights, units, local_sem.at[1])
    load.start()
    gap = jnp.zeros((HD, out_weight.shape[1]), out_weight.dtype)
    for number in range(HEADS):
        block = out_weight[pl.ds(HD * number, HD)]
        for side in range(2):
            spaced[side, pl.ds(BLK * number + HD * side, HD)] = block
            spaced[side, pl.ds(BLK * number + HD * (1 - side), HD)] = gap
    own.wait()
    for copy in copies:
        copy.wait()
    joined = jnp.concatenate([grouped[number] for number in range(HEADS)], 1)
    half = joined.shape[0]
    for side in range(2):
        part = pl.ds(side * half, half)
        attention = jnp.dot(joined, spaced[side], preferred_element_type=jnp.float32)
        residual_sum = features[part].astype(jnp.float32) + attention
        mixed[part] = layer_norm(residual_sum, attn_gain[...])
    hidden_norm = mixed[...].astype(jnp.bfloat16)
    mixed[...] = hidden_norm.astype(jnp.float32)
    load.wait()
    tile = 512
    for step in range(units.shape[1] // tile):
        here = pl.ds(step * tile, tile)
        hidden = lax.dot_general(
            hidden_norm,
            units[0, here],
            (((1,), (1,)), ((), ())),
            preferred_element_type=jnp.float32,
        )
        hidden = jax.nn.gelu(hidden).astype(jnp.bfloat16)
        mixed[...] += jnp.dot(hidden, units[1, here], preferred_element_type=jnp.float32)
    out[...] = layer_norm(mixed[...], final_gain[...]).astype(jnp.bfloat16)


def finish(features, attended, out_weight, attn_gain, weights, final_gain):
    dma = pltpu.SemaphoreType.DMA
    return pl.pallas_call(
        finish_kernel,
        out_shape=jax.ShapeDtypeStruct(features.shape, jnp.bfloat16),
        in_specs=[VMEM] * 4 + [ANY, VMEM],
        out_specs=VMEM,
        scratch_shapes=[
            pltpu.VMEM(attended.shape, jnp.bfloat16),
            pltpu.VMEM((2, HEADS * BLK, features.shape[1]), jnp.bfloat16),
            pltpu.VMEM(weights.shape, jnp.bfloat16),
            pltpu.VMEM(features.shape, jnp.float32),
            dma((HEADS - 1,)),
            dma((HEADS - 1,)),
            dma((2,)),
        ],
        compiler_params=pltpu.CompilerParams(
            collective_id=2, has_side_effects=True, vmem_limit_bytes=LIMIT
        ),
        name="finish_rows",
    )(features, attended, out_weight, attn_gain, weights, final_gain)


def per_device(
    features,
    qkv_weight,
    out_weight,
    attn_gain,
    up_weight,
    down_weight,
    final_gain,
    node_order,
    dest_part,
    key_block,
    row_count,
):
    blocks = dest_part.shape[0]
    partitions = NZ * NX
    width = features.shape[1]
    dom, head = lax.axis_index("dom"), lax.axis_index("head")

    dest_flat, block_flat = dest_part.reshape(-1), key_block.reshape(-1)
    names = dest_flat[:, None] == jnp.arange(partitions, dtype=jnp.int32)[None, :]
    earlier = jnp.tril(dest_flat[:, None] == dest_flat[None, :], -1)
    turn = jnp.sum(earlier.astype(jnp.int32), 1)
    chosen = names[:, :, None] & (turn[:, None, None] == jnp.arange(2, dtype=jnp.int32))
    wanted = jnp.sum(jnp.where(chosen, block_flat[:, None, None], 0), 0).reshape(1, -1)

    picked = lax.dynamic_index_in_dim(
        node_order.reshape(blocks, HEADS, PART), head, 1, keepdims=False
    ).reshape(-1, 1)
    picked = picked - dom * node_order.shape[0]
    own_query, own_pair, slot_pair, weights, tables = exchange(
        features,
        picked,
        up_weight.T,
        down_weight,
        wanted,
        jnp.pad(row_count, (0, wanted.shape[1] - blocks)).reshape(1, -1),
        qkv_weight,
    )
    attended = attend(
        dest_flat,
        block_flat,
        turn,
        row_count,
        tables,
        node_order,
        own_query.reshape(blocks, BLK, BLK),
        own_pair.reshape(blocks, BLK, BLK),
        slot_pair.reshape(2 * partitions, BLK, BLK),
    )
    return finish(
        features,
        attended,
        out_weight,
        attn_gain.reshape(1, width),
        weights.reshape(2, partitions * 2 * PART, width),
        final_gain.reshape(1, width),
    )


def solution(mesh):
    in_specs = (
        P(("dom", "head"), None),
        P(),
        P(),
        P(),
        P(None, "dom"),
        P("dom", None),
        P(),
        P("dom"),
        P("dom", None),
        P("dom", None),
        P("dom"),
    )
    out_specs = P(("dom", "head"), None)
    return jax.shard_map(
        per_device, mesh=mesh, in_specs=in_specs, out_specs=out_specs, check_vma=False
    )
```

time: 561 us -> 224 us (0.40); the launches traced: 551 us -> 223 us
  Pallas kernels: 0 us -> 214 us
  waiting for transfers between devices: 206 us -> 0 us
  local copies, waits for them, and re-layouts: 151 us -> 8.7 us
  matrix products: 64.5 us -> 0 us
  starting transfers between devices: 58.6 us -> 0 us
  blocking collectives: 44.3 us -> 0 us
  between operations: 13.8 us -> 0.12 us
  other arithmetic: 13.3 us -> 0.43 us
    pallas_call x0 -> x3, Pallas kernels: none -> 214 us  [the longest x1 179 us: exchange(): pl.pallas_call(exchange_kernel, out_shape=(jax.ShapeDtypeStruct((blocks,...]
    all_to_all x5 -> x0, waiting for transfers between devices: 189 us -> none  [the longest x1 82.9 us: per_device(): lax.all_to_all(outgoing, 'dom', split_axis=0, concat_axis=0, tiled=True)]
    dot_general x44 -> x0, matrix products: 64.5 us -> none  [the longest x20 33.1 us: attend_core(): jnp.einsum('phqk,pkhe->pqhe', weights.astype(jnp.bfloat16), value_blocks,...]
    all_to_all x5 -> x0, starting transfers between devices: 58 us -> none  [the longest x1 14.8 us: per_device(): lax.all_to_all(outgoing, 'dom', split_axis=0, concat_axis=0, tiled=True)]
    all_to_all x2 -> x0, blocking collectives: 44.3 us -> none  [the longest x1 23.7 us: per_device(): lax.all_to_all(shortened(maxima.reshape(front_shape + (-1,))), 'dom', spl...]
    gather x7 -> x0, local copies, waits for them, and re-layouts: 38.4 us -> none  [the longest x1 30.6 us: per_device(): gathered[:, local_order, :].reshape(3, blocks, BLK, local_heads, HD)]
    slice x1 -> x0, local copies, waits for them, and re-layouts: 28.1 us -> none  [per_device(): query_blocks = clustered[0]]
    another operation x3 -> x0, local copies, waits for them, and re-layouts: 16.6 us -> none  [the longest x1 7.94 us: attend(): query_blocks.reshape((groups, 8) + query_blocks.shape[1:])]
  transfers between devices with their start and end apart: 7 -> 0, of which waited for: 5 -> 0; matrix products, arithmetic and copies ran while one was open for 38% -> 0% of each run, Pallas kernels for 0% -> 0%
where the time goes in v2:
time: 224 us; the launch traced here: 223 us
  Pallas kernels  214 us (96%)
  local copies, waits for them, and re-layouts  8.7 us (4%)
    pallas_call x1, Pallas kernels, exchange(): pl.pallas_call(exchange_kernel, out_shape=(jax.ShapeDtypeStruct((blocks,...  179 us
    pallas_call x1, Pallas kernels, finish(): pl.pallas_call(finish_kernel, out_shape=jax.ShapeDtypeStruct(features.sha...  18.7 us
    pallas_call x1, Pallas kernels, attend(): pl.pallas_call(attend_kernel, out_shape=jax.ShapeDtypeStruct((HEADS, rows...  16 us

profile of v2, /device:TPU:1, one launch (start us, length us, event | category | flops | bytes accessed | tf_op | source)
XLA Modules:
  0.0 223.3 jit_solution(1121411781999225125)
XLA Ops:
  0.0 0.8 reshape.98
  0.8 0.1 subtract_reduce_fusion
  0.9 0.9 sub.11.refs_1_
  1.8 0.8 copy.17
  2.5 0.1 reshape.96.dest
  2.6 0.0 copy-start
  2.6 0.2 convert_reduce_fusion.turn
  2.8 0.0 copy-start.4
  2.8 0.1 iota_compare_fusion
  2.9 0.8 copy.18
  3.7 0.1 reshape.97.key_block
  3.8 0.0 copy-start.1
  3.8 0.1 select_reduce_fusion
  3.9 0.1 copy.19
  4.0 0.7 reshape.99.refs_4_
  4.7 1.2 pad_bitcast_fusion.refs_5_
  5.9 179.4 %exchange_blocks.1 = (bf16[32,8,16,128]{3,2,1,0:T(8,128)(2,1)}, bf16[32,8,16,128]{3,2,1,0:T(8,128)(2,1)}, bf16[128,8,16,128]{3,2,1,0:T(8,128)(2,1)}, bf16[2,4,16...) custom-call(bf16[512,768]{1,0:T(8,128)(2,1)} %features.1, s32[512,1]{1,0:T(8,128)} %sub.11.refs_1_, bf16[24,768]{1,0:T(8,128)(2,1)} %bitcast.11, ...), custom_call_target="tpu_custom_call" | custom-call | tf_op jit(solution)/shard_map/exchange_blocks/pallas_call | solution.py:479
  185.3 0.0 copy-start.2
  185.3 0.0 copy-start.3
  185.3 0.0 copy-done
  185.3 0.0 copy-done.4
  185.3 0.0 copy-done.1
  185.3 16.0 %attend_blocks.1.attended = bf16[8,256,128]{2,1,0:T(8,128)(2,1)} custom-call(s32[64]{0:T(128)} %copy-done, s32[64]{0:T(128)} %copy-done.1, s32[64]{0:T(128)} %copy-done.4, s32[32]{0:T(128)} %row_count.1, s32[64,1,256]{2,1,0:T(1,128)} %get-tuple-element.10.tables, s32[4096]{0:T(1024)} %order.1, bf16[32,128,128]{2,1,0:T(8,128)(2,1)} %bitcast.9, ...), custom_call_target="tpu_custom_call" | custom-call | tf_op jit(solution)/shard_map/attend_blocks/pallas_call | solution.py:601
  201.4 0.0 copy-done.2
  201.4 0.6 reshape.104.attn_gain
  202.0 0.0 copy-done.3
  202.0 0.6 reshape.106.final_gain
  202.6 18.7 %finish_rows.1 = bf16[512,768]{1,0:T(8,128)(2,1)} custom-call(bf16[512,768]{1,0:T(8,128)(2,1)} %features.1, bf16[8,256,128]{2,1,0:T(8,128)(2,1)} %attend_blocks.1.attended, bf16[512,768]{1,0:T(8,128)(2,1)} %out_weight.1, f32[1,768]{1,0:T(1,128)} %reshape.104.attn_gain, bf16[2,2048,768]{2,1,0:T(8,128)(2,1)} %bitcast.7, f32[1,768]{1,0:T(1,128)} %reshape.106.final_gain), custom_call_target="tpu_custom_call" | custom-call | tf_op jit(solution)/shard_map/finish_rows/pallas_call | solution.py:683
  221.3 2.1 copy.22
  (2 shorter events, 0.0 us)
Async XLA Ops:
  2.6 182.7 %copy-start = (s32[64]{0:T(128)}, s32[64]{0:T(128)S(1)}, u32[]{:S(2)}) copy-start(s32[64]{0:T(128)S(1)} %reshape.96.dest) | copy-start | bytes 772
  2.8 182.5 %copy-start.4 = (s32[64]{0:T(128)}, s32[64]{0:T(128)S(1)}, u32[]{:S(2)}) copy-start(s32[64]{0:T(128)S(1)} %convert_reduce_fusion.turn) | copy-start | bytes 772
  3.8 181.5 %copy-start.1 = (s32[64]{0:T(128)}, s32[64]{0:T(128)S(1)}, u32[]{:S(2)}) copy-start(s32[64]{0:T(128)S(1)} %reshape.97.key_block) | copy-start | bytes 772
  185.3 16.1 %copy-start.2 = (f32[768]{0:T(1024)S(1)}, f32[768]{0:T(1024)}, u32[]{:S(2)}) copy-start(f32[768]{0:T(1024)} %param.14) | copy-start | bytes 9220
  185.3 16.7 %copy-start.3 = (f32[768]{0:T(1024)S(1)}, f32[768]{0:T(1024)}, u32[]{:S(2)}) copy-start(f32[768]{0:T(1024)} %param.17) | copy-start | bytes 9220

commit v3 on v2

--- a/solution.py
+++ b/solution.py
@@ -15,6 +15,7 @@
 PART = BLK // HEADS
 HALF_RING = NZ // 2
 FULL_HOPS = 4
+PARTS = 3
 MESH = pl.DeviceIdType.MESH
 VMEM = pl.BlockSpec(memory_space=pltpu.VMEM)
 SMEM = pl.BlockSpec(memory_space=pltpu.SMEM)
@@ -52,8 +53,8 @@
 
 def exchange_kernel(*refs):
     inputs, outputs, scratch = refs[:7], refs[7:12], refs[12:]
-    whole = 4 * FULL_HOPS + 2
-    exchange_body(*inputs, *outputs, scratch[:2], scratch[2:whole], *scratch[whole:])
+    whole = (2 * FULL_HOPS + 1) * PARTS
+    exchange_body(*inputs, *outputs, scratch[:PARTS], scratch[PARTS:whole], *scratch[whole:])
 
 
 def exchange_body(
@@ -107,7 +108,7 @@
     z, x = dom // NX, lax.rem(dom, NX)
     y, core = head // 2, lax.rem(head, 2)
     rows, width = features.shape
-    part_width = width // 2
+    part_width = width // PARTS
 
     def plane(step):
         return lax.rem(z + step + NZ, NZ)
@@ -164,7 +165,8 @@
 
     first_pool = pool_own(0)
     own_table[0, :, : wanted_row.shape[1]] = wanted_row[...]
-    own_table[0, :, wanted_row.shape[1] :] = count_row[...]
+    own_table[0, :, wanted_row.shape[1] :] = jnp.zeros_like(wanted_row)
+    own_table[0, :, pl.ds(wanted_row.shape[1], count_row.shape[1])] = count_row[...]
     table_x = [
         put(own_table, tables.at[pl.ds(dom, 1)], table_send.at[step], table_recv.at[step], rows_x[step])
         for step in range(1, NX)
@@ -229,7 +231,7 @@
 
     def landing(direction, hop, part):
         if hop <= FULL_HOPS:
-            return full[4 * (hop - 1) + 2 * direction + part]
+            return full[PARTS * (2 * (hop - 1) + direction) + part]
         return part_way.at[direction, hop - FULL_HOPS - 1, part]
 
     def ring_go(direction, hop, part):
@@ -270,61 +272,62 @@
 
     slot_copies = {step: [] for step in range(HALF_RING + 1)}
 
-    def slot_go(source, base, step, direction, part, along, count):
-        slot_copies[step].append(
-            put(
-                source,
-                arrived.at[part, pl.ds(base + 2 * (NX - along), count)],
-                row_send.at[step, direction, part, along],
-                row_recv.at[step, direction, part, along],
-                rows_x[along],
+    def slots_pick(step, direction, part):
+        base = slot_base(step) + 8 * direction
+        chunk = landing(direction, step, part) if step else carried[part]
+        source = plane(-step if direction == 0 else step) * NX + x
+        buffer = 2 * step - 1 + direction if step else 0
+        for turn in range(2):
+            arrived[part, base + turn] = chunk[listed(0, x, source, turn)]
+        for along in range(1, NX):
+            for turn in range(2):
+                chosen[buffer, along - 1, part, turn] = chunk[
+                    listed(0, column(along), source, turn)
+                ]
+
+    def slots_along(step, direction):
+        count, base = 2, slot_base(step) + 8 * direction
+        if step > FULL_HOPS:
+            chunk = part_way.at[direction, step - FULL_HOPS - 1]
+            first = 4 + 8 * (HALF_RING - 1 - step)
+            if step == HALF_RING:
+                first, count, base = 0, 1, slot_base(step) + direction
+            arrived[:, pl.ds(base, count)] = chunk[:, pl.ds(first + count * x, count)]
+        for along in range(1, NX):
+            if step > FULL_HOPS:
+                source = chunk.at[:, pl.ds(first + count * column(along), count)]
+            else:
+                source = chosen.at[2 * step - 1 + direction if step else 0, along - 1]
+            slot_copies[step].append(
+                put(
+                    source,
+                    arrived.at[:, pl.ds(base + 2 * (NX - along), count)],
+                    row_send.at[step, direction, along],
+                    row_recv.at[step, direction, along],
+                    rows_x[along],
+                )
             )
-        )
-
-    def slots_along(step, direction, part):
-        base = slot_base(step) + 8 * direction
-        if step <= FULL_HOPS:
-            chunk = landing(direction, step, part) if step else carried[part]
-            source = plane(-step if direction == 0 else step) * NX + x
-            buffer = 2 * step - 1 + direction if step else 0
-            for turn in range(2):
-                arrived[part, base + turn] = chunk[listed(0, x, source, turn)]
-            for along in range(1, NX):
-                for turn in range(2):
-                    chosen[buffer, part, along - 1, turn] = chunk[
-                        listed(0, column(along), source, turn)
-                    ]
-                slot_go(chosen.at[buffer, part, along - 1], base, step, direction, part, along, 2)
-            return
-        chunk = landing(direction, step, part)
-        if step == HALF_RING:
-            first, count, base = 0, 1, slot_base(step) + direction
-        else:
-            first, count = 4 + 8 * (HALF_RING - 1 - step), 2
-        arrived[part, pl.ds(base, count)] = chunk[pl.ds(first + count * x, count)]
-        for along in range(1, NX):
-            source = chunk.at[pl.ds(first + count * column(along), count)]
-            slot_go(source, base, step, direction, part, along, count)
-
-    weight_copies, spread_copies = [], []
-
-    def weights_along(step):
-        if step:
+
+    weight_copies, locals_weights, spread_copies = [], [], []
+
+    def weights_along(turn):
+        some = pl.ds(NZ // NX * turn, NZ // NX)
+        for step in range(1, NX):
             weight_copies.append(
                 put(
-                    weight_column,
-                    weights.at[core, NX - step],
-                    weight_send.at[step],
-                    weight_recv.at[step],
+                    weight_column.at[some],
+                    weights.at[core, NX - step, some],
+                    weight_send.at[turn, step],
+                    weight_recv.at[turn, step],
                     rows_x[step],
                 )
             )
-        else:
-            weight_copies.append(local(weight_column, weights.at[core, 0], 2))
+        locals_weights.append(local(weight_column.at[some], weights.at[core, 0, some], 3 + turn))
 
     def peer_weights():
-        weight_copies[0].wait()
-        for copy in weight_copies[1:]:
+        for copy in locals_weights:
+            copy.wait()
+        for copy in weight_copies:
             copy.wait_recv()
         spread_copies.append(put(weights.at[core], weights.at[core], peer_send, peer_recv, peer))
 
@@ -387,7 +390,7 @@
         def _(step):
             blocks = pl.ds(16 * step, 16)
             joined = jnp.concatenate(
-                [carried[part][blocks].reshape(16 * PART, part_width) for part in range(2)], 1
+                [carried[part][blocks].reshape(16 * PART, part_width) for part in range(PARTS)], 1
             )
             store_queries(joined, sent_own.at[0], 16 * step)
             store_pairs(joined, sent_own.at[1], 16 * step)
@@ -403,14 +406,32 @@
         joined = jnp.concatenate(
             [
                 arrived[part, pl.ds(base, count)].reshape(count * PART, part_width)
-                for part in range(2)
+                for part in range(PARTS)
             ],
             1,
         )
         store_pairs(joined, sent_slot, base)
         spread(sent_slot, slot_pair, step, spread_send, spread_recv, base, count)
 
-    ring, pools, table_z = {}, [first_pool], []
+    ring, pools, table_z, handled = {}, [first_pool], [], set()
+
+    def handle(hop, part):
+        if (hop, part) in handled:
+            return
+        handled.add((hop, part))
+        for direction in range(2):
+            ring[direction, hop, part].wait_recv()
+            if hop == FULL_HOPS:
+                trim(direction, part)
+            if hop < HALF_RING:
+                ring_go(direction, hop + 1, part)
+        if hop <= FULL_HOPS:
+            for direction in range(2):
+                slots_pick(hop, direction, part)
+
+    def begin(part):
+        for direction in range(2):
+            ring_go(direction, 1, part)
 
     def during_first(moment):
         if moment == 0:
@@ -429,33 +450,47 @@
                         planes[step],
                     )
                 )
-        weights_on(moment + 1)
+        if moment in (2, 5):
+            weights_on({2: 1, 5: 2}[moment])
+
+    def during_second(moment):
+        if moment == 0:
+            pools.append(pool_own(2))
+        if moment in (1, 3, 5):
+            weights_on({1: 3, 3: 4, 5: 5}[moment])
+        if moment == 6:
+            handle(1, 0)
+
+    def during_third(moment):
+        if moment in (1, 3, 5):
+            weights_on({1: 6, 3: 7, 5: 8}[moment])
+        if moment == 2:
+            handle(2, 0)
+        if moment == 6:
+            handle(1, 1)
 
     gather_rows(0, pools[0], during_first)
-    for direction in range(2):
-        ring_go(direction, 1, 0)
+    begin(0)
     for copy in table_z:
         copy.wait_recv()
-    local(tables, wanted, 3).wait()
-    slots_along(0, 0, 0)
-    gather_rows(1, pools[1], lambda moment: None)
-    for direction in range(2):
-        ring_go(direction, 1, 1)
-    slots_along(0, 0, 1)
+    local(tables, wanted, 2).wait()
+    slots_pick(0, 0, 0)
+    gather_rows(1, pools[1], during_second)
+    begin(1)
+    slots_pick(0, 0, 1)
+    gather_rows(2, pools[2], during_third)
+    begin(2)
+    slots_pick(0, 0, 2)
+    slots_along(0, 0)
     own_weights.wait()
 
     for hop in range(1, HALF_RING + 1):
-        for part in range(2):
-            for direction in range(2):
-                ring[direction, hop, part].wait_recv()
-                if hop == FULL_HOPS:
-                    trim(direction, part)
-                if hop < HALF_RING:
-                    ring_go(direction, hop + 1, part)
-            for direction in range(2):
-                slots_along(hop, direction, part)
-            if hop == 1 and part == 0:
+        for part in range(PARTS):
+            handle(hop, part)
+            if hop == 1 and part == 1:
                 project_own()
+        for direction in range(2):
+            slots_along(hop, direction)
         if hop <= NX:
             weights_along(hop - 1)
         if hop == HALF_RING - 1:
@@ -472,7 +507,7 @@
 
 def exchange(features, picked, up_rows, down_rows, wanted_row, count_row, qkv_weight):
     rows, width = features.shape
-    blocks, part_width = rows // PART, width // 2
+    blocks, part_width = rows // PART, width // PARTS
     bf16 = jnp.bfloat16
     dma = pltpu.SemaphoreType.DMA
     tables = (NZ * NX, 1, 2 * wanted_row.shape[1])
@@ -487,41 +522,43 @@
         ),
         in_specs=[VMEM] * 7,
         out_specs=(ANY, ANY, ANY, ANY, ANY),
-        scratch_shapes=[pltpu.VMEM((blocks, PART, part_width), bf16)] * (2 + 4 * FULL_HOPS)
+        scratch_shapes=[pltpu.VMEM((blocks, PART, part_width), bf16)]
+        * ((2 * FULL_HOPS + 1) * PARTS)
         + [
-            pltpu.VMEM((2, 8, rows, part_width), bf16),
+            pltpu.VMEM((PARTS, 8, rows, part_width), bf16),
             pltpu.VMEM((rows, part_width), jnp.float32),
             pltpu.VMEM((2, PART, width), bf16),
             pltpu.VMEM((1,) + tables[1:], jnp.int32),
             pltpu.VMEM((NZ, 2, PART, width), bf16),
             pltpu.SMEM(tables, jnp.int32),
             pltpu.VMEM(
-                (2, HALF_RING - FULL_HOPS, 2, hop_size(FULL_HOPS + 1), PART, part_width), bf16
+                (2, HALF_RING - FULL_HOPS, PARTS, hop_size(FULL_HOPS + 1), PART, part_width),
+                bf16,
             ),
-            pltpu.VMEM((2, 2, hop_size(FULL_HOPS + 1), PART, part_width), bf16),
-            pltpu.VMEM((1 + 2 * FULL_HOPS, 2, NX - 1, 2, PART, part_width), bf16),
-            pltpu.VMEM((2, 2 * NZ * NX, PART, part_width), bf16),
+            pltpu.VMEM((2, PARTS, hop_size(FULL_HOPS + 1), PART, part_width), bf16),
+            pltpu.VMEM((1 + 2 * FULL_HOPS, NX - 1, PARTS, 2, PART, part_width), bf16),
+            pltpu.VMEM((PARTS, 2 * NZ * NX, PART, part_width), bf16),
             pltpu.VMEM((2, HEADS, blocks, PART, BLK), bf16),
             pltpu.VMEM((HEADS, 2 * NZ * NX, PART, BLK), bf16),
-            dma((2, 10)),
-            dma((2, 10)),
+            dma((PARTS, 10)),
+            dma((PARTS, 10)),
             dma((NX + NZ,)),
             dma((NX + NZ,)),
             dma((NZ,)),
             dma((NZ,)),
-            dma((2, HALF_RING, 2)),
-            dma((2, HALF_RING, 2)),
-            dma((HALF_RING + 1, 2, 2, NX)),
-            dma((HALF_RING + 1, 2, 2, NX)),
+            dma((2, HALF_RING, PARTS)),
+            dma((2, HALF_RING, PARTS)),
+            dma((HALF_RING + 1, 2, NX)),
+            dma((HALF_RING + 1, 2, NX)),
             dma((HALF_RING + 1, HEADS)),
             dma((HALF_RING + 1, HEADS)),
-            dma((NX,)),
-            dma((NX,)),
+            dma((NX, NX)),
+            dma((NX, NX)),
             dma((2, HEADS)),
             dma((2, HEADS)),
             dma,
             dma,
-            dma((4,)),
+            dma((3 + NX,)),
         ],
         compiler_params=pltpu.CompilerParams(
             collective_id=1, has_side_effects=True, vmem_limit_bytes=LIMIT
@@ -720,11 +757,10 @@
     dom, head = lax.axis_index("dom"), lax.axis_index("head")
 
     dest_flat, block_flat = dest_part.reshape(-1), key_block.reshape(-1)
-    names = dest_flat[:, None] == jnp.arange(partitions, dtype=jnp.int32)[None, :]
     earlier = jnp.tril(dest_flat[:, None] == dest_flat[None, :], -1)
     turn = jnp.sum(earlier.astype(jnp.int32), 1)
-    chosen = names[:, :, None] & (turn[:, None, None] == jnp.arange(2, dtype=jnp.int32))
-    wanted = jnp.sum(jnp.where(chosen, block_flat[:, None, None], 0), 0).reshape(1, -1)
+    entry = (2 * dest_flat + turn)[:, None] == jnp.arange(2 * partitions, dtype=jnp.int32)[None, :]
+    wanted = jnp.sum(jnp.where(entry, block_flat[:, None], 0), 0, keepdims=True)
 
     picked = lax.dynamic_index_in_dim(
         node_order.reshape(blocks, HEADS, PART), head, 1, keepdims=False
@@ -736,7 +772,7 @@
         up_weight.T,
         down_weight,
         wanted,
-        jnp.pad(row_count, (0, wanted.shape[1] - blocks)).reshape(1, -1),
+        row_count.reshape(1, -1),
         qkv_weight,
     )
     attended = attend(

time: 224 us -> 214 us (0.955)
  Pallas kernels: 214 us -> 206 us
    pallas_call x1, Pallas kernels: 179 us -> 171 us  [exchange(): pl.pallas_call(exchange_kernel, out_shape=(jax.ShapeDtypeStruct((blocks,...]
where the time goes in v3:
time: 214 us; the launch traced here: 213 us
  Pallas kernels  206 us (96%)
  local copies, waits for them, and re-layouts  6.68 us (3%)
    pallas_call x1, Pallas kernels, exchange(): pl.pallas_call(exchange_kernel, out_shape=(jax.ShapeDtypeStruct((blocks,...  171 us
    pallas_call x1, Pallas kernels, finish(): pl.pallas_call(finish_kernel, out_shape=jax.ShapeDtypeStruct(features.sha...  18.7 us
    pallas_call x1, Pallas kernels, attend(): pl.pallas_call(attend_kernel, out_shape=jax.ShapeDtypeStruct((HEADS, rows...  16 us

profile of v3, /device:TPU:1, one launch (start us, length us, event | category | flops | bytes accessed | tf_op | source)
XLA Modules:
  0.0 213.5 jit_solution(5325672037783317147)
XLA Ops:
  0.0 0.8 reshape.59
  0.8 0.1 subtract_reduce_fusion
  0.9 0.9 sub.11.refs_1_
  1.8 0.8 copy.17
  2.5 0.1 reshape.57.dest
  2.6 0.0 copy-start
  2.6 0.2 convert_reduce_fusion.turn
  2.8 0.0 copy-start.4
  2.8 0.8 copy.18
  3.6 0.1 reshape.58.key_block
  3.7 0.0 copy-start.3
  3.7 0.7 select_reduce_fusion
  4.4 171.1 %exchange_blocks.1 = (bf16[32,8,16,128]{3,2,1,0:T(8,128)(2,1)}, bf16[32,8,16,128]{3,2,1,0:T(8,128)(2,1)}, bf16[128,8,16,128]{3,2,1,0:T(8,128)(2,1)}, bf16[2,4,16...) custom-call(bf16[512,768]{1,0:T(8,128)(2,1)} %features.1, s32[512,1]{1,0:T(8,128)} %sub.11.refs_1_, bf16[24,768]{1,0:T(8,128)(2,1)} %bitcast.11, ...), custom_call_target="tpu_custom_call" | custom-call | tf_op jit(solution)/shard_map/exchange_blocks/pallas_call | solution.py:514
  175.5 0.0 copy-start.1
  175.5 0.0 copy-start.2
  175.5 0.0 copy-done
  175.5 0.0 copy-done.4
  175.5 0.0 copy-done.3
  175.5 16.0 %attend_blocks.1.attended = bf16[8,256,128]{2,1,0:T(8,128)(2,1)} custom-call(s32[64]{0:T(128)} %copy-done, s32[64]{0:T(128)} %copy-done.3, s32[64]{0:T(128)} %copy-done.4, s32[32]{0:T(128)} %row_count.1, s32[64,1,256]{2,1,0:T(1,128)} %get-tuple-element.10.tables, s32[4096]{0:T(1024)} %order.1, bf16[32,128,128]{2,1,0:T(8,128)(2,1)} %bitcast.9, ...), custom_call_target="tpu_custom_call" | custom-call | tf_op jit(solution)/shard_map/attend_blocks/pallas_call | solution.py:638
  191.5 0.0 copy-done.1
  191.5 0.6 reshape.64.attn_gain
  192.1 0.0 copy-done.2
  192.1 0.6 reshape.66.final_gain
  192.7 18.7 %finish_rows.1 = bf16[512,768]{1,0:T(8,128)(2,1)} custom-call(bf16[512,768]{1,0:T(8,128)(2,1)} %features.1, bf16[8,256,128]{2,1,0:T(8,128)(2,1)} %attend_blocks.1.attended, bf16[512,768]{1,0:T(8,128)(2,1)} %out_weight.1, f32[1,768]{1,0:T(1,128)} %reshape.64.attn_gain, bf16[2,2048,768]{2,1,0:T(8,128)(2,1)} %bitcast.7, f32[1,768]{1,0:T(1,128)} %reshape.66.final_gain), custom_call_target="tpu_custom_call" | custom-call | tf_op jit(solution)/shard_map/finish_rows/pallas_call | solution.py:720
  211.4 2.1 copy.21
  (2 shorter events, 0.0 us)
Async XLA Ops:
  2.6 172.9 %copy-start = (s32[64]{0:T(128)}, s32[64]{0:T(128)S(1)}, u32[]{:S(2)}) copy-start(s32[64]{0:T(128)S(1)} %reshape.57.dest) | copy-start | bytes 772
  2.8 172.7 %copy-start.4 = (s32[64]{0:T(128)}, s32[64]{0:T(128)S(1)}, u32[]{:S(2)}) copy-start(s32[64]{0:T(128)S(1)} %convert_reduce_fusion.turn) | copy-start | bytes 772
  3.7 171.8 %copy-start.3 = (s32[64]{0:T(128)}, s32[64]{0:T(128)S(1)}, u32[]{:S(2)}) copy-start(s32[64]{0:T(128)S(1)} %reshape.58.key_block) | copy-start | bytes 772
  175.5 16.1 %copy-start.1 = (f32[768]{0:T(1024)S(1)}, f32[768]{0:T(1024)}, u32[]{:S(2)}) copy-start(f32[768]{0:T(1024)} %param.14) | copy-start | bytes 9220
  175.5 16.7 %copy-start.2 = (f32[768]{0:T(1024)S(1)}, f32[768]{0:T(1024)}, u32[]{:S(2)}) copy-start(f32[768]{0:T(1024)} %param.17) | copy-start | bytes 9220

commit v4 on v3

--- a/solution.py
+++ b/solution.py
@@ -493,7 +493,7 @@
             slots_along(hop, direction)
         if hop <= NX:
             weights_along(hop - 1)
-        if hop == HALF_RING - 1:
+        if hop == HALF_RING - 2:
             peer_weights()
         project(hop - 1)
     project(HALF_RING)
@@ -697,7 +697,7 @@
         part = pl.ds(side * half, half)
         attention = jnp.dot(joined, spaced[side], preferred_element_type=jnp.float32)
         residual_sum = features[part].astype(jnp.float32) + attention
-        mixed[part] = layer_norm(residual_sum, attn_gain[...])
+        mixed[part] = layer_norm(residual_sum, attn_gain[...].reshape(1, -1))
     hidden_norm = mixed[...].astype(jnp.bfloat16)
     mixed[...] = hidden_norm.astype(jnp.float32)
     load.wait()
@@ -712,7 +712,7 @@
         )
         hidden = jax.nn.gelu(hidden).astype(jnp.bfloat16)
         mixed[...] += jnp.dot(hidden, units[1, here], preferred_element_type=jnp.float32)
-    out[...] = layer_norm(mixed[...], final_gain[...]).astype(jnp.bfloat16)
+    out[...] = layer_norm(mixed[...], final_gain[...].reshape(1, -1)).astype(jnp.bfloat16)
 
 
 def finish(features, attended, out_weight, attn_gain, weights, final_gain):
@@ -790,9 +790,9 @@
         features,
         attended,
         out_weight,
-        attn_gain.reshape(1, width),
+        attn_gain,
         weights.reshape(2, partitions * 2 * PART, width),
-        final_gain.reshape(1, width),
+        final_gain,
     )
 
 

time: 214 us -> 213 us (level)
  no operation moved by 1% of the time
where the time goes in v4:
time: 213 us; the launch traced here: 212 us
  Pallas kernels  206 us (97%)
  local copies, waits for them, and re-layouts  5.47 us (3%)
    pallas_call x1, Pallas kernels, exchange(): pl.pallas_call(exchange_kernel, out_shape=(jax.ShapeDtypeStruct((blocks,...  171 us
    pallas_call x1, Pallas kernels, finish(): pl.pallas_call(finish_kernel, out_shape=jax.ShapeDtypeStruct(features.sha...  18.7 us
    pallas_call x1, Pallas kernels, attend(): pl.pallas_call(attend_kernel, out_shape=jax.ShapeDtypeStruct((HEADS, rows...  16 us

profile of v4, /device:TPU:1, one launch (start us, length us, event | category | flops | bytes accessed | tf_op | source)
XLA Modules:
  0.0 212.3 jit_solution(16937883989503123539)
XLA Ops:
  0.0 0.8 copy.17
  0.8 0.1 reshape.51.dest
  0.9 0.0 copy-start
  0.9 0.2 convert_reduce_fusion.turn
  1.1 0.0 copy-start.2
  1.1 0.8 copy.18
  1.8 0.1 reshape.52.key_block
  1.9 0.0 copy-start.1
  2.0 0.7 select_reduce_fusion
  2.6 0.8 reshape.53
  3.5 0.1 subtract_reduce_fusion
  3.5 0.9 sub.11.refs_1_
  4.4 171.1 %exchange_blocks.1 = (bf16[32,8,16,128]{3,2,1,0:T(8,128)(2,1)}, bf16[32,8,16,128]{3,2,1,0:T(8,128)(2,1)}, bf16[128,8,16,128]{3,2,1,0:T(8,128)(2,1)}, bf16[2,4,16...) custom-call(bf16[512,768]{1,0:T(8,128)(2,1)} %features.1, s32[512,1]{1,0:T(8,128)} %sub.11.refs_1_, bf16[24,768]{1,0:T(8,128)(2,1)} %bitcast.11, ...), custom_call_target="tpu_custom_call" | custom-call | tf_op jit(solution)/shard_map/exchange_blocks/pallas_call | solution.py:514
  175.4 0.0 copy-done
  175.5 0.0 copy-done.2
  175.5 0.0 copy-done.1
  175.5 16.0 %attend_blocks.1.attended = bf16[8,256,128]{2,1,0:T(8,128)(2,1)} custom-call(s32[64]{0:T(128)} %copy-done, s32[64]{0:T(128)} %copy-done.1, s32[64]{0:T(128)} %copy-done.2, s32[32]{0:T(128)} %row_count.1, s32[64,1,256]{2,1,0:T(1,128)} %get-tuple-element.10.tables, s32[4096]{0:T(1024)} %order.1, bf16[32,128,128]{2,1,0:T(8,128)(2,1)} %bitcast.9, ...), custom_call_target="tpu_custom_call" | custom-call | tf_op jit(solution)/shard_map/attend_blocks/pallas_call | solution.py:638
  191.5 18.7 %finish_rows.1 = bf16[512,768]{1,0:T(8,128)(2,1)} custom-call(bf16[512,768]{1,0:T(8,128)(2,1)} %features.1, bf16[8,256,128]{2,1,0:T(8,128)(2,1)} %attend_blocks.1.attended, bf16[512,768]{1,0:T(8,128)(2,1)} %out_weight.1, f32[768]{0:T(1024)} %attn_gain.1, bf16[2,2048,768]{2,1,0:T(8,128)(2,1)} %bitcast.7, f32[768]{0:T(1024)} %final_gain.1), custom_call_target="tpu_custom_call" | custom-call | tf_op jit(solution)/shard_map/finish_rows/pallas_call | solution.py:720
  210.2 2.1 copy.21
  (2 shorter events, 0.0 us)
Async XLA Ops:
  0.9 174.6 %copy-start = (s32[64]{0:T(128)}, s32[64]{0:T(128)S(1)}, u32[]{:S(2)}) copy-start(s32[64]{0:T(128)S(1)} %reshape.51.dest) | copy-start | bytes 772
  1.1 174.4 %copy-start.2 = (s32[64]{0:T(128)}, s32[64]{0:T(128)S(1)}, u32[]{:S(2)}) copy-start(s32[64]{0:T(128)S(1)} %convert_reduce_fusion.turn) | copy-start | bytes 772
  1.9 173.5 %copy-start.1 = (s32[64]{0:T(128)}, s32[64]{0:T(128)S(1)}, u32[]{:S(2)}) copy-start(s32[64]{0:T(128)S(1)} %reshape.52.key_block) | copy-start | bytes 772
